TPU v7x, 512 devices: a whole 4x4x16 slice. The times are simulated.
512 devices in a mesh: grp: 16 (over z_lo, core), dev: 32 (over z_hi, x, y).
Axes of the slice: x: 4, y: 4, z: 16 (z_hi: 2, z_lo: 8; z = z_hi * 8 + z_lo), core: 2. Of those that a mesh axis runs over, the one named last changes fastest.
Arguments:
- embeddings: float32 [131072, 1280], P(('grp', 'dev')), may hold values from -6 to 6
- factor: float32 [131072, 512], P(('grp', 'dev')), may hold values from -0.078125 to 0.078125
- pivots: int32 [512], replicated, may hold values from 0 to 131071, as said below
Outputs:
- new_factor: float32 [131072, 512], P(('grp', 'dev'))
- core_columns: float32 [1024, 512], P('dev')
Inputs may be any that keep to these rules, and one draw needn't show every extreme that they name: The pivots are distinct row indices. The rows of one device (256 consecutive rows) hold at most 3 pivots and some device holds exactly 3; the rows of one index of grp hold at most 48 pivots and some index holds exactly 48.
All inputs are finite; a program needn't handle non-finite values.
Results may differ from a plain program's by a relative error of at most 0.00022.
Values sent between devices are 32-bit elements; how exact they have to be, the bound alone decides.
No kernel may reach another device: no remote copies, remote signals or barrier semaphores. Data moves between devices by JAX's collectives and lax.ppermute only.
A program may use at most 128 MiB of HBM per device.

v0:
```python
import jax
import jax.numpy as jnp
from jax import lax
from jax.sharding import PartitionSpec as P

ridge_term = 1.0
core_ridge = 1.0


def kernel_tile(left, right, width):
    left_sq = jnp.sum(left * left, axis=1)
    right_sq = jnp.sum(right * right, axis=1)
    cross = jnp.dot(
        left, right.T, precision=lax.Precision.HIGHEST, preferred_element_type=jnp.float32
    )
    return jnp.exp(-(left_sq[:, None] + right_sq[None, :] - 2.0 * cross) / (2.0 * width))


def same_before(labels):
    order = jnp.arange(labels.shape[0])
    same = (labels[None, :] == labels[:, None]) & (order[None, :] < order[:, None])
    return jnp.sum(same.astype(jnp.int32), axis=1)


def pick_slots(owned, slot_rank, n_slots, values):
    hit = owned[None, :] & (slot_rank[None, :] == jnp.arange(n_slots)[:, None])
    picked = jnp.sum(jnp.where(hit, values[None, :], 0), axis=1)
    present = jnp.any(hit, axis=1)
    return (picked, present)


def on_device(embeddings, factor, pivots):
    rows_dev, width = embeddings.shape
    old_rank = factor.shape[1]
    count_piv = pivots.shape[0]
    n_grp = lax.axis_size("grp")
    n_dev = lax.axis_size("dev")
    p_max = max(2, 3 * count_piv // (n_grp * n_dev))
    my_grp = lax.axis_index("grp")
    my_dev = lax.axis_index("dev")
    mine = my_grp * n_dev + my_dev
    owner = pivots // rows_dev
    rank_dev = same_before(owner)
    own_rows = jnp.concatenate([embeddings, factor], axis=1)
    local_index, present = pick_slots(owner == mine, rank_dev, p_max, pivots - mine * rows_dev)
    packed = jnp.take(own_rows, local_index, axis=0) * present[:, None].astype(jnp.float32)
    gathered = lax.all_gather(packed, ("grp", "dev"), axis=0, tiled=True)
    chosen_rows = jnp.take(gathered, owner * p_max + rank_dev, axis=0)
    chosen = chosen_rows[:, :width]
    chosen_factor = chosen_rows[:, width:]
    pivot_block = kernel_tile(chosen, chosen, width) - jnp.dot(
        chosen_factor,
        chosen_factor.T,
        precision=lax.Precision.HIGHEST,
        preferred_element_type=jnp.float32,
    )
    pivot_block = pivot_block + ridge_term * jnp.eye(count_piv, dtype=jnp.float32)
    lower = jnp.linalg.cholesky(pivot_block)
    residual_tile = kernel_tile(embeddings, chosen, width) - jnp.dot(
        factor, chosen_factor.T, precision=lax.Precision.HIGHEST, preferred_element_type=jnp.float32
    )
    new_factor = lax.linalg.triangular_solve(
        lower, residual_tile, left_side=False, lower=True, transpose_a=True
    )
    full_factor = jnp.concatenate([factor, new_factor], axis=1)
    partial_core = lax.dot_general(
        full_factor,
        new_factor,
        (((0,), (0,)), ((), ())),
        precision=lax.Precision.HIGHEST,
        preferred_element_type=jnp.float32,
    )
    share_rows = (old_rank + count_piv) // n_dev
    summed = lax.psum(partial_core, "grp")
    core_share = lax.psum_scatter(summed, "dev", scatter_dimension=0, tiled=True)
    global_rows = my_dev * share_rows + jnp.arange(share_rows)
    diagonal_hit = global_rows[:, None] - old_rank == jnp.arange(count_piv)[None, :]
    core_columns = core_share + core_ridge * diagonal_hit.astype(jnp.float32)
    return (new_factor, core_columns)


def solution(mesh):
    in_specs = (P(("grp", "dev"), None), P(("grp", "dev"), None), P())
    out_specs = (P(("grp", "dev"), None), P("dev", None))
    return jax.shard_map(
        on_device, mesh=mesh, in_specs=in_specs, out_specs=out_specs, check_vma=False
    )
```

profile of v0, /device:TPU:1, one launch (start us, length us, event | category | flops | bytes accessed | tf_op | source)
XLA Modules:
  0.0 2151.7 jit_solution(12932088086083978666)
XLA Ops:
  9.3 2.9 pad_maximum_fusion
  16.1 1436.0 %all-gather.3.cloned.1.call-done = f32[512,3,1792]{2,1,0:T(4,128)} async-done(((f32[1,3,1792]{2,1,0:T(4,128)}), f32[512,3,1792]{2,1,0:T(4,128)}) %all-gather.3.cloned.1.call-update) | async-done | bytes 11010064 | tf_op jit(solution)/shard_map/all_gather | solution.py:47
  1452.1 16.4 reshape.117
  1468.5 9.5 gather_fusion.1
  1478.0 2.3 broadcast_select_fusion
  1482.5 6.1 broadcast_add_fusion
  1488.6 2.6 copy.32
  1491.1 2.5 copy.33
  1495.0 2.8 fusion.28
  1498.8 11.9 cholesky.104
  1510.8 9.8 custom-call.30
  1523.2 11.7 cholesky.217
  1534.9 9.8 custom-call.31
  1546.3 11.9 cholesky.238
  1558.9 9.8 custom-call.32
  1570.1 11.7 cholesky.255
  1586.8 11.2 while.1
  1587.3 2.2 bitcast_dynamic-update-slice_fusion.2
  1597.9 39.6 %custom-call.33 = f32[4,128,128]{1,2,0:T(8,128)S(1)} custom-call(f32[4,128,128]{2,1,0:T(8,128)S(1)} %get-tuple-element.9), custom_call_target="InvertDiagBlocksLowerTriangular" | custom-call | tf_op jit(solution)/shard_map/triangular_solve | solution.py:62
  1637.5 4.0 fusion.23
  1641.5 2.3 fusion.13
  1649.3 4.8 fusion.68
  1654.2 291.9 %reduce-scatter.2.cloned.1.call-done = f32[32,512]{1,0:T(8,128)} async-done(((f32[1024,512]{1,0:T(8,128)}), f32[32,512]{1,0:T(8,128)}) %reduce-scatter.2.cloned.1.call-update) | async-done | bytes 65552 | tf_op jit(solution)/shard_map/reduce_scatter | solution.py:75
  1947.1 196.3 %all-reduce.3.cloned.1.call-done = f32[32,512]{1,0:T(8,128)} async-done(((f32[32,512]{1,0:T(8,128)}), f32[32,512]{1,0:T(8,128)}) %all-reduce.3.cloned.1.call-update) | async-done | bytes 65552 | tf_op jit(solution)/shard_map/psum | solution.py:74
  (85 shorter events, 36.0 us)
Async XLA Ops:
  7.2 8.7 copy-start.1
  7.2 7.9 copy-start.2
  7.2 1444.9 %all-gather.3.cloned.1.call-start = ((), (), s32[]{:S(2)}) async-start(), calls=%async_computation.3 | async-start | bytes 14708736 | tf_op jit(solution)/shard_map/all_gather | solution.py:47
  14.9 1931.1 %reduce-scatter.2.cloned.1.call-start = ((), (), s32[]{:S(2)}) async-start(), calls=%async_computation.1 | async-start | bytes 2162688 | tf_op jit(solution)/shard_map/reduce_scatter | solution.py:75
  1480.4 8.2 copy-start
  1497.8 1.0 copy-start.3
  1641.5 7.7 copy-start.4
  1654.1 489.3 %all-reduce.3.cloned.1.call-start = ((), (), s32[]{:S(2)}) async-start(), calls=%async_computation.2 | async-start | bytes 131072 | tf_op jit(solution)/shard_map/psum | solution.py:74
Sparse Core Ops, SparseCore 0:
  15.1 1436.9 all-gather.2
  1654.2 291.7 reduce-scatter.1
  1949.2 194.1 all-reduce.2
where the time goes:
time: 2160 us; the launch traced here: 2150 us
  waiting for transfers between devices  1920 us (89%)
  other arithmetic  132 us (6%)
  local copies, waits for them, and re-layouts  48.9 us (2%)
  matrix products  29.4 us (1%)
    all_gather x1, waiting for transfers between devices, on_device(): gathered = lax.all_gather(packed, ('grp', 'dev'), axis=0, tiled=True)  1440 us
    reduce_scatter x1, waiting for transfers between devices, on_device(): lax.psum_scatter(summed, 'dev', scatter_dimension=0, tiled=True)  292 us
    psum x1, waiting for transfers between devices, on_device(): summed = lax.psum(partial_core, 'grp')  196 us
    another operation x14, other arithmetic, on_device(): lower = jnp.linalg.cholesky(pivot_block)  78.7 us
  transfers between devices with their start and end apart: 3, of which 3 were waited for; matrix products, arithmetic and copies ran while one was open for 0% of the time, Pallas kernels for 0%

commit v1 on v0

v1 whole, which is shorter than its diff:
```python
import functools

import jax
import jax.numpy as jnp
from jax import lax
from jax.experimental import pallas as pl
from jax.experimental.pallas import tpu as pltpu
from jax.sharding import Mesh
from jax.sharding import PartitionSpec as P

ridge_term = 1.0
core_ridge = 1.0

SLOTS = 3
BLOCK = 128
PANEL = 8
f32 = jnp.float32
bf16 = jnp.bfloat16


def split2(a):
    high = a.astype(bf16)
    return high, (a - high.astype(f32)).astype(bf16)


def split3(a):
    high = a.astype(bf16)
    rest = a - high.astype(f32)
    mid = rest.astype(bf16)
    return high, mid, (rest - mid.astype(f32)).astype(bf16)


def mul(a, b, dims):
    return lax.dot_general(a, b, (dims, ((), ())), preferred_element_type=f32)


def mul3(a, b, dims):
    (ah, al), (bh, bl) = a, b
    return mul(ah, bh, dims) + (mul(ah, bl, dims) + mul(al, bh, dims))


NN = ((1,), (0,))
NT = ((1,), (1,))
TN = ((0,), (0,))


def pick_kernel(width, place_ref, pivots_ref, emb_ref, fac_ref, out_ref):
    base, core = place_ref[0], place_ref[1]
    rows_dev = emb_ref.shape[0]
    count = pivots_ref.shape[1]
    local = (pivots_ref[...] - base).astype(f32)
    order = lax.broadcasted_iota(jnp.int32, (1, count), 1).astype(f32)
    inside = jnp.where((local >= 0) & (local < rows_dev), 1.0, 0.0)
    sub = lax.broadcasted_iota(jnp.int32, (8, rows_dev), 0)
    lane = lax.broadcasted_iota(jnp.int32, (8, rows_dev), 1).astype(f32)
    sub_tag = lax.broadcasted_iota(jnp.int32, (8, BLOCK), 0)
    hot = jnp.zeros((8, rows_dev), f32)
    tag = jnp.full((8, BLOCK), -1.0, f32)
    for k in range(SLOTS):
        pos = jnp.min(jnp.where(inside > 0, order, float(count)), axis=1, keepdims=True)
        hit = order == pos
        row = jnp.sum(jnp.where(hit, local, 0.0), axis=1, keepdims=True)
        valid = pos < count
        row = jnp.where(valid, row, -1.0)
        hot = hot + jnp.where((sub == k) & (lane == row), 1.0, 0.0)
        tag = jnp.where((sub_tag == k), jnp.where(valid, pos, -1.0), tag)
        inside = jnp.where(hit, 0.0, inside)
    hot = hot.astype(bf16)
    pieces = []
    for ref in (emb_ref, fac_ref):
        for c in range(0, ref.shape[1], 256):
            high, mid, low = split3(ref[:, c : c + 256])
            pieces.append(mul(hot, high, NN) + (mul(hot, mid, NN) + mul(hot, low, NN)))
    rows = jnp.concatenate(pieces + [jnp.zeros((8, BLOCK), f32)], axis=1)
    lane_out = lax.broadcasted_iota(jnp.int32, (8, BLOCK), 1)
    for j in range(out_ref.shape[0]):
        first = width * j
        tile = first // BLOCK * BLOCK
        window = rows[:, tile : tile + 2 * BLOCK]
        if first > tile:
            window = pltpu.roll(window, 2 * BLOCK - (first - tile), 1)
        piece = jnp.where(lane_out < width, window[:, :BLOCK], jnp.where(lane_out == width, tag, 0.0))
        piece = jnp.where(core == 0, piece, pltpu.roll(piece, BLOCK // 2, 1))
        out_ref[j] = piece


def select_kernel(width, slots_ref, out_ref):
    slots = slots_ref[...]
    count = out_ref.shape[1]
    order = lax.broadcasted_iota(jnp.int32, (1, count), 1).astype(f32)
    half = BLOCK // 2
    parts = split3(slots)
    total = None
    for c in range(2):
        tag = slots[:, c * half + width : c * half + width + 1]
        hot = jnp.where(tag == order, 1.0, 0.0).astype(bf16)
        for part in parts:
            got = mul(part, hot, TN)[c * half : c * half + width]
            total = got if total is None else total + got
    out_ref[...] = total


def factor_block(mat_ref, off, inv_ref, d_ref, e_ref):
    d_ref[...] = mat_ref[pl.ds(off, BLOCK), pl.ds(off, BLOCK)]
    e_ref[...] = jnp.where(
        lax.broadcasted_iota(jnp.int32, (BLOCK, BLOCK), 0)
        == lax.broadcasted_iota(jnp.int32, (BLOCK, BLOCK), 1),
        1.0,
        0.0,
    ).astype(f32)
    full = (PANEL, BLOCK)

    def spread(a, lane):
        return jnp.broadcast_to(a[:, lane : lane + 1], full)

    for p in range(BLOCK // PANEL):
        first = p * PANEL
        rows = [jnp.broadcast_to(d_ref[first + k : first + k + 1, :], full) for k in range(PANEL)]
        invs = [jnp.broadcast_to(e_ref[first + k : first + k + 1, :], full) for k in range(PANEL)]
        s = [[spread(rows[i], first + k) for k in range(i + 1)] for i in range(PANEL)]
        scale = []
        for k in range(PANEL):
            r = lax.rsqrt(s[k][k])
            scale.append(r)
            for i in range(k + 1, PANEL):
                s[i][k] = s[i][k] * r
            for i in range(k + 1, PANEL):
                for j in range(k + 1, i + 1):
                    s[i][j] = s[i][j] - s[i][k] * s[j][k]
        for k in range(PANEL):
            for m in range(k):
                rows[k] = rows[k] - s[k][m] * rows[m]
                invs[k] = invs[k] - s[k][m] * invs[m]
            rows[k] = rows[k] * scale[k]
            invs[k] = invs[k] * scale[k]
            inv_ref[first + k : first + k + 1, :] = invs[k][0:1, :]
        for b in range(p + 1, BLOCK // PANEL):
            at = slice(b * PANEL, (b + 1) * PANEL)
            d = d_ref[at, :]
            e = e_ref[at, :]
            cols = [spread(d, first + k) for k in range(PANEL)]
            for k in range(PANEL):
                for m in range(k):
                    cols[k] = cols[k] - s[k][m] * cols[m]
                cols[k] = cols[k] * scale[k]
            for k in range(PANEL):
                d = d - cols[k] * rows[k]
                e = e - cols[k] * invs[k]
            d_ref[at, :] = d
            e_ref[at, :] = e


def main_kernel(
    place_ref, emb_ref, fac_ref, own_ref, other_ref, new_ref, keep_ref, send_ref,
    ch_ref, cl_ref, sq_ref, mat_ref, inv_ref, d_ref, e_ref, sum_ref,
):
    core = place_ref[1]
    rows_dev, width = emb_ref.shape
    old_rank = fac_ref.shape[1]
    half, count = own_ref.shape
    total = 2 * half
    second = width - half
    scale = 1.0 / (2.0 * width)

    def take(ref, which):
        start = pl.multiple_of(which * half, BLOCK)
        sq = jnp.zeros((1, count), f32)
        for r in range(0, half, BLOCK):
            a = ref[r : r + BLOCK, :]
            high, low = split2(a)
            at = pl.ds(pl.multiple_of(start + r, BLOCK), BLOCK)
            ch_ref[at, :] = high
            cl_ref[at, :] = low
            part = jnp.sum(a * a, axis=0, keepdims=True)
            if r >= second:
                part = jnp.where(which == 0, part, 0.0)
            sq = sq + part
        return sq

    sq = take(own_ref, core) + take(other_ref, 1 - core)
    sq_ref[...] = jnp.transpose(jnp.broadcast_to(sq, (BLOCK, count)))

    def wide(lo, hi):
        return ch_ref[lo:hi, :], cl_ref[lo:hi, :]

    for i in range(count // BLOCK):
        at = slice(i * BLOCK, (i + 1) * BLOCK)
        cross = mul3((ch_ref[:width, at], cl_ref[:width, at]), wide(0, width), TN)
        old = mul3((ch_ref[width:, at], cl_ref[width:, at]), wide(width, total), TN)
        left = sq_ref[at, 0:1]
        block = jnp.exp((2.0 * cross - (left + sq)) * scale) - old
        row = lax.broadcasted_iota(jnp.int32, (BLOCK, count), 0) + i * BLOCK
        col = lax.broadcasted_iota(jnp.int32, (BLOCK, count), 1)
        mat_ref[at, :] = block + jnp.where(row == col, ridge_term, 0.0)
    for i in range(rows_dev // BLOCK):
        at = slice(i * BLOCK, (i + 1) * BLOCK)
        a = emb_ref[at, :]
        cross = mul3(split2(a), wide(0, width), NN)
        old = mul3(split2(fac_ref[at, :]), wide(width, total), NN)
        left = jnp.sum(a * a, axis=1, keepdims=True)
        mat_ref[count + i * BLOCK : count + (i + 1) * BLOCK, :] = (
            jnp.exp((2.0 * cross - (left + sq)) * scale) - old
        )

    all_rows = count + rows_dev

    def step(kb, carry):
        off = pl.multiple_of(kb * BLOCK, BLOCK)
        factor_block(mat_ref, off, inv_ref, d_ref, e_ref)
        panel = mul3(split2(mat_ref[:, pl.ds(off, BLOCK)]), split2(inv_ref[...]), NT)
        new_ref[:, pl.ds(off, BLOCK)] = panel[count:]
        row = lax.broadcasted_iota(jnp.int32, (all_rows, BLOCK), 0)
        panel = jnp.where(row >= off + BLOCK, panel, 0.0)
        high, low = split2(panel)
        for r in range(0, all_rows, 256):
            mat_ref[r : r + 256, :] = mat_ref[r : r + 256, :] - mul3(
                (high[r : r + 256], low[r : r + 256]), (high[:count], low[:count]), NT
            )
        return carry

    lax.fori_loop(0, count // BLOCK, step, 0)

    new = split2(new_ref[...])
    for i in range(old_rank // BLOCK):
        at = slice(i * BLOCK, (i + 1) * BLOCK)
        sum_ref[at, :] = mul3(split2(fac_ref[:, at]), new, TN)
    for i in range(count // BLOCK):
        at = slice(i * BLOCK, (i + 1) * BLOCK)
        sum_ref[old_rank + i * BLOCK : old_rank + (i + 1) * BLOCK, :] = mul3(
            (new[0][:, at], new[1][:, at]), new, TN
        )
    _, n_zh, part, _ = keep_ref.shape
    shares = keep_ref.shape[0]
    for zh in range(n_zh):
        for j in range(shares):
            start = (zh * shares + j) * 2 * part
            keep_ref[j, zh] = sum_ref[pl.ds(pl.multiple_of(start + core * part, part), part), :]
            send_ref[j, zh] = sum_ref[pl.ds(pl.multiple_of(start + (1 - core) * part, part), part), :]


VMEM = pl.BlockSpec(memory_space=pltpu.VMEM)
SMEM = pl.BlockSpec(memory_space=pltpu.SMEM)
PARAMS = pltpu.CompilerParams(vmem_limit_bytes=48 * 1024 * 1024)


def on_device(n_xy, n_z, embeddings, factor, pivots):
    rows_dev, width = embeddings.shape
    old_rank = factor.shape[1]
    count = pivots.shape[0]
    total = width + old_rank
    slices = 2 * n_xy
    piece = total // slices
    core = lax.axis_index("core")
    mine = lax.axis_index(("zl", "core", "zh", "x", "y"))
    place = jnp.stack([mine * rows_dev, core]).astype(jnp.int32)
    sent = pl.pallas_call(
        functools.partial(pick_kernel, piece),
        out_shape=jax.ShapeDtypeStruct((slices, 8, BLOCK), f32),
        in_specs=[SMEM, VMEM, VMEM, VMEM],
        out_specs=VMEM,
        compiler_params=PARAMS,
        name="pick",
    )(place, pivots.reshape(1, count), embeddings, factor)
    got = lax.all_to_all(sent, ("core", "x", "y"), 0, 0, tiled=True)
    packed = (got[:n_xy] + got[n_xy:])[:, :SLOTS].reshape(n_xy * SLOTS, BLOCK)
    packed = jnp.broadcast_to(packed[None], (n_z, n_xy * SLOTS, BLOCK))
    slots = lax.all_to_all(packed, ("zl", "zh"), 0, 0, tiled=True)
    chosen_slice = pl.pallas_call(
        functools.partial(select_kernel, piece),
        out_shape=jax.ShapeDtypeStruct((piece, count), f32),
        in_specs=[VMEM],
        out_specs=VMEM,
        compiler_params=PARAMS,
        name="select",
    )(slots.reshape(n_z * n_xy * SLOTS, BLOCK))
    wide = jnp.broadcast_to(chosen_slice[None], (n_xy, piece, count))
    own = lax.all_to_all(wide, ("x", "y"), 0, 0, tiled=True).reshape(n_xy * piece, count)
    other = lax.ppermute(own, "core", [(0, 1), (1, 0)])
    share = (old_rank + count) // slices
    part = share // 2
    split = jax.ShapeDtypeStruct((n_xy, 2, part, count), f32)
    new_factor, keep, send = pl.pallas_call(
        main_kernel,
        out_shape=(jax.ShapeDtypeStruct((rows_dev, count), f32), split, split),
        in_specs=[SMEM, VMEM, VMEM, VMEM, VMEM],
        out_specs=(VMEM, VMEM, VMEM),
        scratch_shapes=[
            pltpu.VMEM((total, count), bf16),
            pltpu.VMEM((total, count), bf16),
            pltpu.VMEM((count, BLOCK), f32),
            pltpu.VMEM((count + rows_dev, count), f32),
            pltpu.VMEM((BLOCK, BLOCK), f32),
            pltpu.VMEM((BLOCK, BLOCK), f32),
            pltpu.VMEM((BLOCK, BLOCK), f32),
            pltpu.VMEM((old_rank + count, count), f32),
        ],
        compiler_params=PARAMS,
        name="main",
    )(place, embeddings, factor, own, other)
    pair = keep + lax.ppermute(send, "core", [(0, 1), (1, 0)])
    layer = jnp.sum(lax.all_to_all(pair, ("x", "y"), 0, 0, tiled=True), axis=0)
    spread = jnp.broadcast_to(layer[None], (n_z // 2, 2, part, count)).reshape(n_z, part, count)
    summed = jnp.sum(lax.all_to_all(spread, ("zl", "zh"), 0, 0, tiled=True), axis=0)
    core_share = lax.all_gather(summed, "core", axis=0, tiled=True)
    my_dev = lax.axis_index(("zh", "x", "y"))
    global_rows = my_dev * share + jnp.arange(share)
    diagonal_hit = global_rows[:, None] - old_rank == jnp.arange(count)[None, :]
    return new_factor, core_share + core_ridge * diagonal_hit.astype(f32)


def solution(mesh):
    n_zl, n_zh, n_x = 8, 2, 4
    n_y = mesh.shape["dev"] // (n_zh * n_x)
    n_core = mesh.shape["grp"] // n_zl
    axes = ("zl", "core", "zh", "x", "y")
    fine = Mesh(mesh.devices.reshape(n_zl, n_core, n_zh, n_x, n_y), axes)
    in_specs = (P(axes, None), P(axes, None), P())
    out_specs = (P(axes, None), P(("zh", "x", "y"), None))
    return jax.shard_map(
        functools.partial(on_device, n_x * n_y, n_zl * n_zh),
        mesh=fine, in_specs=in_specs, out_specs=out_specs, check_vma=False,
    )
```

time: 2160 us -> 195 us (0.09)
  waiting for transfers between devices: 1920 us -> 30.1 us
  other arithmetic: 132 us -> 1.12 us
  blocking collectives: 0 us -> 105 us
  local copies, waits for them, and re-layouts: 48.9 us -> 5.42 us
  Pallas kernels: 0 us -> 34.3 us
  matrix products: 29.4 us -> 0 us
    all_gather x1 -> x0, waiting for transfers between devices: 1440 us -> none  [on_device(): gathered = lax.all_gather(packed, ('grp', 'dev'), axis=0, tiled=True)]
    reduce_scatter x1 -> x0, waiting for transfers between devices: 292 us -> none  [on_device(): lax.psum_scatter(summed, 'dev', scatter_dimension=0, tiled=True)]
    psum x1 -> x0, waiting for transfers between devices: 196 us -> none  [on_device(): summed = lax.psum(partial_core, 'grp')]
    another operation x18 -> x1, other arithmetic: 119 us -> 0.08 us  [on_device(): place = jnp.stack([mine * rows_dev, core]).astype(jnp.int32)]
    all_to_all x0 -> x4, blocking collectives: none -> 96.6 us  [the longest x1 34.8 us: on_device(): slots = lax.all_to_all(packed, ('zl', 'zh'), 0, 0, tiled=True)]
    pallas_call x0 -> x3, Pallas kernels: none -> 34.3 us  [the longest x1 31.9 us: on_device(): pl.pallas_call(main_kernel, out_shape=(jax.ShapeDtypeStruct((rows_dev, co...]
    all_to_all x0 -> x1, waiting for transfers between devices: none -> 24.6 us  [on_device(): lax.all_to_all(spread, ('zl', 'zh'), 0, 0, tiled=True)]
where the time goes in v1:
time: 195 us; the launch traced here: 193 us
  blocking collectives  105 us (54%)
  Pallas kernels  34.3 us (18%)
  waiting for transfers between devices  30.1 us (15%)
  starting transfers between devices  16.8 us (9%)
  local copies, waits for them, and re-layouts  5.42 us (3%)
    all_to_all x1, blocking collectives, on_device(): slots = lax.all_to_all(packed, ('zl', 'zh'), 0, 0, tiled=True)  34.8 us
    pallas_call x1, Pallas kernels, on_device(): pl.pallas_call(main_kernel, out_shape=(jax.ShapeDtypeStruct((rows_dev, co...  31.9 us
    all_to_all x1, blocking collectives, on_device(): lax.all_to_all(wide, ('x', 'y'), 0, 0, tiled=True)  25.4 us
    all_to_all x1, waiting for transfers between devices, on_device(): lax.all_to_all(spread, ('zl', 'zh'), 0, 0, tiled=True)  24.6 us
    all_to_all x1, blocking collectives, on_device(): layer = jnp.sum(lax.all_to_all(pair, ('x', 'y'), 0, 0, tiled=True), axis=0)  19.3 us
    all_to_all x1, blocking collectives, on_device(): got = lax.all_to_all(sent, ('core', 'x', 'y'), 0, 0, tiled=True)  17.1 us
    all_gather x1, blocking collectives, on_device(): core_share = lax.all_gather(summed, 'core', axis=0, tiled=True)  7.92 us
    all_to_all x1, starting transfers between devices, on_device(): lax.all_to_all(spread, ('zl', 'zh'), 0, 0, tiled=True)  7.89 us
  transfers between devices with their start and end apart: 3, of which 3 were waited for; matrix products, arithmetic and copies ran while one was open for 0% of the time, Pallas kernels for 0%

profile of v1, /device:TPU:1, one launch (start us, length us, event | category | flops | bytes accessed | tf_op | source)
XLA Modules:
  0.0 193.1 jit_solution(18441140871382103526)
XLA Ops:
  0.6 0.1 pad_add_fusion.place_ref
  0.7 1.3 copy-done
  2.0 1.0 copy-done.2
  3.1 0.7 copy-done.4
  3.8 1.5 pick.1
  5.3 17.1 %all_to_all.25 = f32[32,8,128]{2,1,0:T(8,128)S(1)} all-to-all(f32[32,8,128]{2,1,0:T(8,128)S(1)} %pick.1), channel_id=1, replica_groups=mesh['zl'=8,'core'=2,'zh'=2,'x'=4,'y'=4] {'core','x','y'}, dimensions={0} | all-to-all | bytes 262144 | tf_op jit(solution)/shard_map/all_to_all | solution.py:264
  22.5 34.8 %all_to_all.26 = f32[16,48,128]{2,1,0:T(8,128)S(1)} all-to-all(f32[16,48,128]{2,1,0:T(8,128)S(1)} %broadcast_in_dim.9), channel_id=1, replica_groups=mesh['zl'=8,'core'=2,'zh'=2,'x'=4,'y'=4] {'zl','zh'}, dimensions={0} | all-to-all | bytes 786432 | tf_op jit(solution)/shard_map/all_to_all | solution.py:267
  57.3 0.9 select.1
  58.3 0.2 broadcast_in_dim.10
  58.5 25.4 %all_to_all.27 = f32[16,56,512]{2,1,0:T(8,128)S(1)} all-to-all(f32[16,56,512]{2,1,0:T(8,128)S(1)} %broadcast_in_dim.10), channel_id=1, replica_groups=mesh['zl'=8,'core'=2,'zh'=2,'x'=4,'y'=4] {'x','y'}, dimensions={0} | all-to-all | bytes 3670016 | tf_op jit(solution)/shard_map/all_to_all | solution.py:277
  83.9 6.7 %collective-permute-start = (f32[896,512]{1,0:T(8,128)S(1)}, f32[896,512]{1,0:T(8,128)S(1)}, u32[]{:S(2)}, u32[]{:S(2)}) collective-permute-start(f32[896,512]{1,0:T(8,128)S(1)} %bitcast.6), channel_id=1, source_target_pairs={{0,32},{32,0},{1,33},{33,1},{2,34},{34,2},{3,35},{35,3},{4,36},{36... | collective-permute-start | bytes 5505032 | tf_op jit(solution)/shard_map/ppermute | solution.py:278
  90.6 3.2 %collective-permute-done.other_ref = f32[896,512]{1,0:T(8,128)S(1)} collective-permute-done((f32[896,512]{1,0:T(8,128)S(1)}, f32[896,512]{1,0:T(8,128)S(1)}, u32[]{:S(2)}, u32[]{:S(2)}) %collective-permute-start) | collective-permute-done | bytes 1835040 | tf_op jit(solution)/shard_map/ppermute | solution.py:278
  93.8 1.2 copy-done.5
  95.1 31.9 %main.1 = (f32[256,512]{1,0:T(8,128)}, f32[16,2,16,512]{3,2,1,0:T(8,128)S(1)}, f32[16,2,16,512]{3,2,1,0:T(8,128)S(1)}) custom-call(s32[2]{0:T(128)S(1)} %pad_add_fusion.place_ref, f32[256,1280]{1,0:T(8,128)S(1)} %copy-done.1, f32[256,512]{1,0:T(8,128)S(1)} %copy-done.3, f32[896,512]{1,0:T(8,128)S(1)} %bitcast.7, f32[896,512]{1,0:T(8,128)} %copy-done.5), custom_call_target="tpu_custom_call" | custom-call | tf_op jit(solution)/shard_map/main/pallas_call | solution.py:282
  127.0 2.3 %collective-permute-start.1 = (f32[16,2,16,512]{3,2,1,0:T(8,128)S(1)}, f32[16,2,16,512]{3,2,1,0:T(8,128)S(1)}, u32[]{:S(2)}, u32[]{:S(2)}) collective-permute-start(f32[16,2,16,512]{3,2,1,0:T(8,128)S(1)} %get-tuple-element.7), channel_id=1, source_target_pairs={{0,32},{32,0},{1,33},{33,1},{2,34},{34,2},{3,35},{35,3},{4,36},{36... | collective-permute-start | bytes 3145736 | tf_op jit(solution)/shard_map/ppermute | solution.py:300
  129.2 2.3 %collective-permute-done.1 = f32[16,2,16,512]{3,2,1,0:T(8,128)S(1)} collective-permute-done((f32[16,2,16,512]{3,2,1,0:T(8,128)S(1)}, f32[16,2,16,512]{3,2,1,0:T(8,128)S(1)}, u32[]{:S(2)}, u32[]{:S(2)}) %collective-permute-start.1) | collective-permute-done | bytes 1048608 | tf_op jit(solution)/shard_map/ppermute | solution.py:300
  131.5 0.2 add.44
  131.7 19.3 %all_to_all.28 = f32[16,2,16,512]{3,2,1,0:T(8,128)S(1)} all-to-all(f32[16,2,16,512]{3,2,1,0:T(8,128)S(1)} %add.44), channel_id=1, replica_groups=mesh['zl'=8,'core'=2,'zh'=2,'x'=4,'y'=4] {'x','y'}, dimensions={0} | all-to-all | bytes 2097152 | tf_op jit(solution)/shard_map/all_to_all | solution.py:301
  151.0 0.1 reduce_sum.18
  151.0 0.9 broadcast_in_dim.11
  151.9 7.9 %all-to-all-start.4 = ((f32[16,16,512]{2,1,0:T(8,128)}), f32[16,16,512]{2,1,0:T(8,128)S(1)}, u32[]{:S(2)}, u32[]{:S(2)}) async-start(f32[16,16,512]{2,1,0:T(8,128)} %bitcast.5), calls=%async_computation.4 | async-start | bytes 1048576 | tf_op jit(solution)/shard_map/all_to_all | solution.py:303
  159.8 24.6 %all-to-all-done.4 = f32[16,16,512]{2,1,0:T(8,128)S(1)} async-done(((f32[16,16,512]{2,1,0:T(8,128)}), f32[16,16,512]{2,1,0:T(8,128)S(1)}, u32[]{:S(2)}, u32[]{:S(2)}) %all-to-all-start.4) | async-done | bytes 524320 | tf_op jit(solution)/shard_map/all_to_all | solution.py:303
  184.5 7.9 %all_gather.3 = f32[32,512]{1,0:T(8,128)S(1)} all-gather(f32[16,512]{1,0:T(8,128)S(1)} %reduce_sum.19), channel_id=1, replica_groups=mesh['zl'=8,'core'=2,'zh'=2,'x'=4,'y'=4] {'core'}, dimensions={0}, use_global_device_ids=true | all-gather | bytes 98304 | tf_op jit(solution)/shard_map/all_gather | solution.py:304
  192.4 0.7 convert_add_fusion
  (14 shorter events, 0.1 us)
Async XLA Ops:
  0.7 1.3 copy-start
  2.0 1.0 copy-start.2
  3.1 0.7 copy-start.4
  58.5 36.6 %copy-start.1 = (f32[256,1280]{1,0:T(8,128)S(1)}, f32[256,1280]{1,0:T(8,128)}, u32[]{:S(2)}) copy-start(f32[256,1280]{1,0:T(8,128)} %emb_ref.3) | copy-start | bytes 3932164
  58.5 36.6 %copy-start.3 = (f32[256,512]{1,0:T(8,128)S(1)}, f32[256,512]{1,0:T(8,128)}, u32[]{:S(2)}) copy-start(f32[256,512]{1,0:T(8,128)} %fac_ref.3) | copy-start | bytes 1572868
  83.9 9.9 %collective-permute-start = (f32[896,512]{1,0:T(8,128)S(1)}, f32[896,512]{1,0:T(8,128)S(1)}, u32[]{:S(2)}, u32[]{:S(2)}) collective-permute-start(f32[896,512]{1,0:T(8,128)S(1)} %bitcast.6), channel_id=1, source_target_pairs={{0,32},{32,0},{1,33},{33,1},{2,34},{34,2},{3,35},{35,3},{4,36},{36... | collective-permute-start | bytes 5505032 | tf_op jit(solution)/shard_map/ppermute | solution.py:278
  93.8 1.2 copy-start.5
  127.0 4.5 %collective-permute-start.1 = (f32[16,2,16,512]{3,2,1,0:T(8,128)S(1)}, f32[16,2,16,512]{3,2,1,0:T(8,128)S(1)}, u32[]{:S(2)}, u32[]{:S(2)}) collective-permute-start(f32[16,2,16,512]{3,2,1,0:T(8,128)S(1)} %get-tuple-element.7), channel_id=1, source_target_pairs={{0,32},{32,0},{1,33},{33,1},{2,34},{34,2},{3,35},{35,3},{4,36},{36... | collective-permute-start | bytes 3145736 | tf_op jit(solution)/shard_map/ppermute | solution.py:300
  151.9 32.5 %all-to-all-start.4 = ((f32[16,16,512]{2,1,0:T(8,128)}), f32[16,16,512]{2,1,0:T(8,128)S(1)}, u32[]{:S(2)}, u32[]{:S(2)}) async-start(f32[16,16,512]{2,1,0:T(8,128)} %bitcast.5), calls=%async_computation.4 | async-start | bytes 1048576 | tf_op jit(solution)/shard_map/all_to_all | solution.py:303

commit v2 on v1

--- a/solution.py
+++ b/solution.py
@@ -180,23 +180,24 @@
     sq = take(own_ref, core) + take(other_ref, 1 - core)
     sq_ref[...] = jnp.transpose(jnp.broadcast_to(sq, (BLOCK, count)))
 
-    def wide(lo, hi):
-        return ch_ref[lo:hi, :], cl_ref[lo:hi, :]
+    def wide(lo, hi, need):
+        return ch_ref[lo:hi, :need], cl_ref[lo:hi, :need]
 
     for i in range(count // BLOCK):
         at = slice(i * BLOCK, (i + 1) * BLOCK)
-        cross = mul3((ch_ref[:width, at], cl_ref[:width, at]), wide(0, width), TN)
-        old = mul3((ch_ref[width:, at], cl_ref[width:, at]), wide(width, total), TN)
+        need = (i // 2 + 1) * 2 * BLOCK
+        cross = mul3((ch_ref[:width, at], cl_ref[:width, at]), wide(0, width, need), TN)
+        old = mul3((ch_ref[width:, at], cl_ref[width:, at]), wide(width, total, need), TN)
         left = sq_ref[at, 0:1]
-        block = jnp.exp((2.0 * cross - (left + sq)) * scale) - old
-        row = lax.broadcasted_iota(jnp.int32, (BLOCK, count), 0) + i * BLOCK
-        col = lax.broadcasted_iota(jnp.int32, (BLOCK, count), 1)
-        mat_ref[at, :] = block + jnp.where(row == col, ridge_term, 0.0)
+        block = jnp.exp((2.0 * cross - (left + sq[:, :need])) * scale) - old
+        row = lax.broadcasted_iota(jnp.int32, (BLOCK, need), 0) + i * BLOCK
+        col = lax.broadcasted_iota(jnp.int32, (BLOCK, need), 1)
+        mat_ref[at, :need] = block + jnp.where(row == col, ridge_term, 0.0)
     for i in range(rows_dev // BLOCK):
         at = slice(i * BLOCK, (i + 1) * BLOCK)
         a = emb_ref[at, :]
-        cross = mul3(split2(a), wide(0, width), NN)
-        old = mul3(split2(fac_ref[at, :]), wide(width, total), NN)
+        cross = mul3(split2(a), wide(0, width, count), NN)
+        old = mul3(split2(fac_ref[at, :]), wide(width, total, count), NN)
         left = jnp.sum(a * a, axis=1, keepdims=True)
         mat_ref[count + i * BLOCK : count + (i + 1) * BLOCK, :] = (
             jnp.exp((2.0 * cross - (left + sq)) * scale) - old
@@ -213,9 +214,14 @@
         panel = jnp.where(row >= off + BLOCK, panel, 0.0)
         high, low = split2(panel)
         for r in range(0, all_rows, 256):
-            mat_ref[r : r + 256, :] = mat_ref[r : r + 256, :] - mul3(
-                (high[r : r + 256], low[r : r + 256]), (high[:count], low[:count]), NT
-            )
+            for c in range(0, min(r + 256, count), 256):
+
+                @pl.when(off + BLOCK < min(r, c) + 256)
+                def _():
+                    mat_ref[r : r + 256, c : c + 256] = mat_ref[r : r + 256, c : c + 256] - mul3(
+                        (high[r : r + 256], low[r : r + 256]), (high[c : c + 256], low[c : c + 256]), NT
+                    )
+
         return carry
 
     lax.fori_loop(0, count // BLOCK, step, 0)
@@ -299,9 +305,13 @@
     )(place, embeddings, factor, own, other)
     pair = keep + lax.ppermute(send, "core", [(0, 1), (1, 0)])
     layer = jnp.sum(lax.all_to_all(pair, ("x", "y"), 0, 0, tiled=True), axis=0)
-    spread = jnp.broadcast_to(layer[None], (n_z // 2, 2, part, count)).reshape(n_z, part, count)
+    n_zl = n_z // 2
+    few = part // n_zl
+    spread = jnp.swapaxes(layer.reshape(2, n_zl, few, count), 0, 1).reshape(n_z, few, count)
     summed = jnp.sum(lax.all_to_all(spread, ("zl", "zh"), 0, 0, tiled=True), axis=0)
-    core_share = lax.all_gather(summed, "core", axis=0, tiled=True)
+    line = jnp.broadcast_to(summed[None], (n_zl, few, count))
+    line = lax.all_to_all(line, "zl", 0, 0, tiled=True).reshape(part, count)
+    core_share = lax.all_gather(line, "core", axis=0, tiled=True)
     my_dev = lax.axis_index(("zh", "x", "y"))
     global_rows = my_dev * share + jnp.arange(share)
     diagonal_hit = global_rows[:, None] - old_rank == jnp.arange(count)[None, :]

time: 195 us -> 189 us (0.969)
  blocking collectives: 105 us -> 123 us
  waiting for transfers between devices: 30.1 us -> 14.9 us
  starting transfers between devices: 16.8 us -> 12.3 us
  Pallas kernels: 34.3 us -> 31.6 us
    all_to_all x0 -> x1, blocking collectives: none -> 19.8 us  [on_device(): lax.all_to_all(spread, ('zl', 'zh'), 0, 0, tiled=True)]
    all_to_all x1, waiting for transfers between devices: 24.6 us -> 9.41 us  [on_device(): line = lax.all_to_all(line, 'zl', 0, 0, tiled=True).reshape(part, count)]
    all_to_all x1, starting transfers between devices: 7.89 us -> 3.34 us  [on_device(): line = lax.all_to_all(line, 'zl', 0, 0, tiled=True).reshape(part, count)]
    pallas_call x1, Pallas kernels: 31.9 us -> 29.2 us  [on_device(): pl.pallas_call(main_kernel, out_shape=(jax.ShapeDtypeStruct((rows_dev, co...]
where the time goes in v2:
time: 189 us
  blocking collectives  123 us (65%)
  Pallas kernels  31.6 us (17%)
  waiting for transfers between devices  14.9 us (8%)
  starting transfers between devices  12.3 us (7%)
  local copies, waits for them, and re-layouts  5.3 us (3%)
    all_to_all x1, blocking collectives, on_device(): slots = lax.all_to_all(packed, ('zl', 'zh'), 0, 0, tiled=True)  34.8 us
    pallas_call x1, Pallas kernels, on_device(): pl.pallas_call(main_kernel, out_shape=(jax.ShapeDtypeStruct((rows_dev, co...  29.2 us
    all_to_all x1, blocking collectives, on_device(): lax.all_to_all(wide, ('x', 'y'), 0, 0, tiled=True)  25.4 us
    all_to_all x1, blocking collectives, on_device(): lax.all_to_all(spread, ('zl', 'zh'), 0, 0, tiled=True)  19.8 us
    all_to_all x1, blocking collectives, on_device(): layer = jnp.sum(lax.all_to_all(pair, ('x', 'y'), 0, 0, tiled=True), axis=0)  19.3 us
    all_to_all x1, blocking collectives, on_device(): got = lax.all_to_all(sent, ('core', 'x', 'y'), 0, 0, tiled=True)  17.1 us
    all_to_all x1, waiting for transfers between devices, on_device(): line = lax.all_to_all(line, 'zl', 0, 0, tiled=True).reshape(part, count)  9.41 us
    ppermute x1, starting transfers between devices, on_device(): other = lax.ppermute(own, 'core', [(0, 1), (1, 0)])  6.7 us
  transfers between devices with their start and end apart: 3, of which 3 were waited for; matrix products, arithmetic and copies ran while one was open for 0% of the time, Pallas kernels for 0%

profile of v2, /device:TPU:1, one launch (start us, length us, event | category | flops | bytes accessed | tf_op | source)
XLA Modules:
  0.0 188.7 jit_solution(17596835547789437623)
XLA Ops:
  0.6 0.1 pad_add_fusion.place_ref
  0.7 1.3 copy-done
  2.0 1.0 copy-done.2
  3.1 0.7 copy-done.4
  3.8 1.5 pick.1
  5.3 17.1 %all_to_all.30 = f32[32,8,128]{2,1,0:T(8,128)S(1)} all-to-all(f32[32,8,128]{2,1,0:T(8,128)S(1)} %pick.1), channel_id=1, replica_groups=mesh['zl'=8,'core'=2,'zh'=2,'x'=4,'y'=4] {'core','x','y'}, dimensions={0} | all-to-all | bytes 262144 | tf_op jit(solution)/shard_map/all_to_all | solution.py:270
  22.5 34.8 %all_to_all.31 = f32[16,48,128]{2,1,0:T(8,128)S(1)} all-to-all(f32[16,48,128]{2,1,0:T(8,128)S(1)} %broadcast_in_dim.9), channel_id=1, replica_groups=mesh['zl'=8,'core'=2,'zh'=2,'x'=4,'y'=4] {'zl','zh'}, dimensions={0} | all-to-all | bytes 786432 | tf_op jit(solution)/shard_map/all_to_all | solution.py:273
  57.3 0.9 select.1
  58.3 0.2 broadcast_in_dim.10
  58.5 25.4 %all_to_all.32 = f32[16,56,512]{2,1,0:T(8,128)S(1)} all-to-all(f32[16,56,512]{2,1,0:T(8,128)S(1)} %broadcast_in_dim.10), channel_id=1, replica_groups=mesh['zl'=8,'core'=2,'zh'=2,'x'=4,'y'=4] {'x','y'}, dimensions={0} | all-to-all | bytes 3670016 | tf_op jit(solution)/shard_map/all_to_all | solution.py:283
  83.9 6.7 %collective-permute-start = (f32[896,512]{1,0:T(8,128)S(1)}, f32[896,512]{1,0:T(8,128)S(1)}, u32[]{:S(2)}, u32[]{:S(2)}) collective-permute-start(f32[896,512]{1,0:T(8,128)S(1)} %bitcast.9), channel_id=1, source_target_pairs={{0,32},{32,0},{1,33},{33,1},{2,34},{34,2},{3,35},{35,3},{4,36},{36... | collective-permute-start | bytes 5505032 | tf_op jit(solution)/shard_map/ppermute | solution.py:284
  90.6 3.2 %collective-permute-done.other_ref = f32[896,512]{1,0:T(8,128)S(1)} collective-permute-done((f32[896,512]{1,0:T(8,128)S(1)}, f32[896,512]{1,0:T(8,128)S(1)}, u32[]{:S(2)}, u32[]{:S(2)}) %collective-permute-start) | collective-permute-done | bytes 1835040 | tf_op jit(solution)/shard_map/ppermute | solution.py:284
  93.8 1.2 copy-done.5
  95.1 29.2 %main.1 = (f32[256,512]{1,0:T(8,128)}, f32[16,2,16,512]{3,2,1,0:T(8,128)S(1)}, f32[16,2,16,512]{3,2,1,0:T(8,128)S(1)}) custom-call(s32[2]{0:T(128)S(1)} %pad_add_fusion.place_ref, f32[256,1280]{1,0:T(8,128)S(1)} %copy-done.1, f32[256,512]{1,0:T(8,128)S(1)} %copy-done.3, f32[896,512]{1,0:T(8,128)S(1)} %bitcast.10, f32[896,512]{1,0:T(8,128)} %copy-done.5), custom_call_target="tpu_custom_call" | custom-call | tf_op jit(solution)/shard_map/main/pallas_call | solution.py:288
  124.3 2.3 %collective-permute-start.1 = (f32[16,2,16,512]{3,2,1,0:T(8,128)S(1)}, f32[16,2,16,512]{3,2,1,0:T(8,128)S(1)}, u32[]{:S(2)}, u32[]{:S(2)}) collective-permute-start(f32[16,2,16,512]{3,2,1,0:T(8,128)S(1)} %get-tuple-element.7), channel_id=1, source_target_pairs={{0,32},{32,0},{1,33},{33,1},{2,34},{34,2},{3,35},{35,3},{4,36},{36... | collective-permute-start | bytes 3145736 | tf_op jit(solution)/shard_map/ppermute | solution.py:306
  126.6 2.3 %collective-permute-done.1 = f32[16,2,16,512]{3,2,1,0:T(8,128)S(1)} collective-permute-done((f32[16,2,16,512]{3,2,1,0:T(8,128)S(1)}, f32[16,2,16,512]{3,2,1,0:T(8,128)S(1)}, u32[]{:S(2)}, u32[]{:S(2)}) %collective-permute-start.1) | collective-permute-done | bytes 1048608 | tf_op jit(solution)/shard_map/ppermute | solution.py:306
  128.9 0.2 add.44
  129.1 19.3 %all_to_all.33 = f32[16,2,16,512]{3,2,1,0:T(8,128)S(1)} all-to-all(f32[16,2,16,512]{3,2,1,0:T(8,128)S(1)} %add.44), channel_id=1, replica_groups=mesh['zl'=8,'core'=2,'zh'=2,'x'=4,'y'=4] {'x','y'}, dimensions={0} | all-to-all | bytes 2097152 | tf_op jit(solution)/shard_map/all_to_all | solution.py:307
  148.5 19.8 %all_to_all.34 = f32[16,2,512]{2,1,0:T(2,128)S(1)} all-to-all(f32[16,2,512]{2,1,0:T(2,128)S(1)} %bitcast.14), channel_id=1, replica_groups=mesh['zl'=8,'core'=2,'zh'=2,'x'=4,'y'=4] {'zl','zh'}, dimensions={0} | all-to-all | bytes 131072 | tf_op jit(solution)/shard_map/all_to_all | solution.py:311
  168.3 0.6 broadcast_in_dim.11
  169.0 3.3 %all-to-all-start.5 = ((f32[8,2,512]{2,1,0:T(2,128)}), f32[8,2,512]{2,1,0:T(2,128)S(1)}, u32[]{:S(2)}, u32[]{:S(2)}) async-start(f32[8,2,512]{2,1,0:T(2,128)} %broadcast_in_dim.11), calls=%async_computation.5 | async-start | bytes 65536 | tf_op jit(solution)/shard_map/all_to_all | solution.py:313
  172.3 9.4 %all-to-all-done.5 = f32[8,2,512]{2,1,0:T(2,128)S(1)} async-done(((f32[8,2,512]{2,1,0:T(2,128)}), f32[8,2,512]{2,1,0:T(2,128)S(1)}, u32[]{:S(2)}, u32[]{:S(2)}) %all-to-all-start.5) | async-done | bytes 32800 | tf_op jit(solution)/shard_map/all_to_all | solution.py:313
  181.8 6.3 %all_gather.3 = f32[32,512]{1,0:T(8,128)S(1)} all-gather(f32[16,512]{1,0:T(8,128)S(1)} %reshape.36), channel_id=1, replica_groups=mesh['zl'=8,'core'=2,'zh'=2,'x'=4,'y'=4] {'core'}, dimensions={0}, use_global_device_ids=true | all-gather | bytes 98304 | tf_op jit(solution)/shard_map/all_gather | solution.py:314
  188.0 0.7 convert_add_fusion
  (18 shorter events, 0.3 us)
Async XLA Ops:
  0.7 1.3 copy-start
  2.0 1.0 copy-start.2
  3.1 0.7 copy-start.4
  58.5 36.6 %copy-start.1 = (f32[256,1280]{1,0:T(8,128)S(1)}, f32[256,1280]{1,0:T(8,128)}, u32[]{:S(2)}) copy-start(f32[256,1280]{1,0:T(8,128)} %emb_ref.3) | copy-start | bytes 3932164
  58.5 36.6 %copy-start.3 = (f32[256,512]{1,0:T(8,128)S(1)}, f32[256,512]{1,0:T(8,128)}, u32[]{:S(2)}) copy-start(f32[256,512]{1,0:T(8,128)} %fac_ref.3) | copy-start | bytes 1572868
  83.9 9.9 %collective-permute-start = (f32[896,512]{1,0:T(8,128)S(1)}, f32[896,512]{1,0:T(8,128)S(1)}, u32[]{:S(2)}, u32[]{:S(2)}) collective-permute-start(f32[896,512]{1,0:T(8,128)S(1)} %bitcast.9), channel_id=1, source_target_pairs={{0,32},{32,0},{1,33},{33,1},{2,34},{34,2},{3,35},{35,3},{4,36},{36... | collective-permute-start | bytes 5505032 | tf_op jit(solution)/shard_map/ppermute | solution.py:284
  93.8 1.2 copy-start.5
  124.3 4.5 %collective-permute-start.1 = (f32[16,2,16,512]{3,2,1,0:T(8,128)S(1)}, f32[16,2,16,512]{3,2,1,0:T(8,128)S(1)}, u32[]{:S(2)}, u32[]{:S(2)}) collective-permute-start(f32[16,2,16,512]{3,2,1,0:T(8,128)S(1)} %get-tuple-element.7), channel_id=1, source_target_pairs={{0,32},{32,0},{1,33},{33,1},{2,34},{34,2},{3,35},{35,3},{4,36},{36... | collective-permute-start | bytes 3145736 | tf_op jit(solution)/shard_map/ppermute | solution.py:306
  169.0 12.8 %all-to-all-start.5 = ((f32[8,2,512]{2,1,0:T(2,128)}), f32[8,2,512]{2,1,0:T(2,128)S(1)}, u32[]{:S(2)}, u32[]{:S(2)}) async-start(f32[8,2,512]{2,1,0:T(2,128)} %broadcast_in_dim.11), calls=%async_computation.5 | async-start | bytes 65536 | tf_op jit(solution)/shard_map/all_to_all | solution.py:313

commit v3 on v2

--- a/solution.py
+++ b/solution.py
@@ -44,7 +44,18 @@
 TN = ((0,), (0,))
 
 
-def pick_kernel(width, place_ref, pivots_ref, emb_ref, fac_ref, out_ref):
+def pick_kernel(
+    width, place_ref, pivots_hbm, emb_hbm, fac_hbm, out_ref, pivots_ref, emb_ref, fac_ref, sems
+):
+    copies = [
+        pltpu.make_async_copy(src, dst, sems.at[i])
+        for i, (src, dst) in enumerate(
+            ((pivots_hbm, pivots_ref), (emb_hbm, emb_ref), (fac_hbm, fac_ref))
+        )
+    ]
+    for copy in copies:
+        copy.start()
+    copies[0].wait()
     base, core = place_ref[0], place_ref[1]
     rows_dev = emb_ref.shape[0]
     count = pivots_ref.shape[1]
@@ -67,7 +78,8 @@
         inside = jnp.where(hit, 0.0, inside)
     hot = hot.astype(bf16)
     pieces = []
-    for ref in (emb_ref, fac_ref):
+    for ref, copy in ((emb_ref, copies[1]), (fac_ref, copies[2])):
+        copy.wait()
         for c in range(0, ref.shape[1], 256):
             high, mid, low = split3(ref[:, c : c + 256])
             pieces.append(mul(hot, high, NN) + (mul(hot, mid, NN) + mul(hot, low, NN)))
@@ -246,7 +258,9 @@
 
 VMEM = pl.BlockSpec(memory_space=pltpu.VMEM)
 SMEM = pl.BlockSpec(memory_space=pltpu.SMEM)
-PARAMS = pltpu.CompilerParams(vmem_limit_bytes=48 * 1024 * 1024)
+HBM = pl.BlockSpec(memory_space=pltpu.HBM)
+PARAMS = pltpu.CompilerParams(vmem_limit_bytes=24 * 1024 * 1024)
+WIDE_PARAMS = pltpu.CompilerParams(vmem_limit_bytes=60 * 1024 * 1024)
 
 
 def on_device(n_xy, n_z, embeddings, factor, pivots):
@@ -262,9 +276,15 @@
     sent = pl.pallas_call(
         functools.partial(pick_kernel, piece),
         out_shape=jax.ShapeDtypeStruct((slices, 8, BLOCK), f32),
-        in_specs=[SMEM, VMEM, VMEM, VMEM],
+        in_specs=[SMEM, HBM, HBM, HBM],
         out_specs=VMEM,
-        compiler_params=PARAMS,
+        scratch_shapes=[
+            pltpu.VMEM((1, count), jnp.int32),
+            pltpu.VMEM((rows_dev, width), f32),
+            pltpu.VMEM((rows_dev, old_rank), f32),
+            pltpu.SemaphoreType.DMA((3,)),
+        ],
+        compiler_params=WIDE_PARAMS,
         name="pick",
     )(place, pivots.reshape(1, count), embeddings, factor)
     got = lax.all_to_all(sent, ("core", "x", "y"), 0, 0, tiled=True)
@@ -309,13 +329,13 @@
     few = part // n_zl
     spread = jnp.swapaxes(layer.reshape(2, n_zl, few, count), 0, 1).reshape(n_z, few, count)
     summed = jnp.sum(lax.all_to_all(spread, ("zl", "zh"), 0, 0, tiled=True), axis=0)
+    my_dev = lax.axis_index(("zh", "x", "y"))
+    first = my_dev * share + core * part + lax.axis_index("zl") * few
+    diagonal_hit = first + jnp.arange(few)[:, None] - old_rank == jnp.arange(count)[None, :]
+    summed = summed + core_ridge * diagonal_hit.astype(f32)
     line = jnp.broadcast_to(summed[None], (n_zl, few, count))
     line = lax.all_to_all(line, "zl", 0, 0, tiled=True).reshape(part, count)
-    core_share = lax.all_gather(line, "core", axis=0, tiled=True)
-    my_dev = lax.axis_index(("zh", "x", "y"))
-    global_rows = my_dev * share + jnp.arange(share)
-    diagonal_hit = global_rows[:, None] - old_rank == jnp.arange(count)[None, :]
-    return new_factor, core_share + core_ridge * diagonal_hit.astype(f32)
+    return new_factor, lax.all_gather(line, "core", axis=0, tiled=True)
 
 
 def solution(mesh):

time: 189 us -> 186 us (0.984)
  blocking collectives: 123 us -> 115 us
  starting transfers between devices: 12.3 us -> 16.9 us
  local copies, waits for them, and re-layouts: 5.3 us -> 1.67 us
  waiting for transfers between devices: 14.9 us -> 17.6 us
    all_to_all x1, blocking collectives: 19.8 us -> 11.9 us  [on_device(): line = lax.all_to_all(line, 'zl', 0, 0, tiled=True).reshape(part, count)]
    all_to_all x1, starting transfers between devices: 3.34 us -> 7.89 us  [on_device(): lax.all_to_all(spread, ('zl', 'zh'), 0, 0, tiled=True)]
    unnamed x12 -> x7, local copies, waits for them, and re-layouts: 4.29 us -> 0.65 us
    all_to_all x1, waiting for transfers between devices: 9.41 us -> 12.1 us  [on_device(): lax.all_to_all(spread, ('zl', 'zh'), 0, 0, tiled=True)]
    pallas_call x1, Pallas kernels: 1.5 us -> 3.54 us  [on_device(): pl.pallas_call(functools.partial(pick_kernel, piece), out_shape=jax.Shape...]
where the time goes in v3:
time: 186 us; the launch traced here: 185 us
  blocking collectives  115 us (62%)
  Pallas kernels  32.6 us (18%)
  waiting for transfers between devices  17.6 us (9%)
  starting transfers between devices  16.9 us (9%)
    all_to_all x1, blocking collectives, on_device(): slots = lax.all_to_all(packed, ('zl', 'zh'), 0, 0, tiled=True)  34.2 us
    pallas_call x1, Pallas kernels, on_device(): pl.pallas_call(main_kernel, out_shape=(jax.ShapeDtypeStruct((rows_dev, co...  28.1 us
    all_to_all x1, blocking collectives, on_device(): lax.all_to_all(wide, ('x', 'y'), 0, 0, tiled=True)  25.4 us
    all_to_all x1, blocking collectives, on_device(): layer = jnp.sum(lax.all_to_all(pair, ('x', 'y'), 0, 0, tiled=True), axis=0)  19.3 us
    all_to_all x1, blocking collectives, on_device(): got = lax.all_to_all(sent, ('core', 'x', 'y'), 0, 0, tiled=True)  18 us
    all_to_all x1, waiting for transfers between devices, on_device(): lax.all_to_all(spread, ('zl', 'zh'), 0, 0, tiled=True)  12.1 us
    all_to_all x1, blocking collectives, on_device(): line = lax.all_to_all(line, 'zl', 0, 0, tiled=True).reshape(part, count)  11.9 us
    all_to_all x1, starting transfers between devices, on_device(): lax.all_to_all(spread, ('zl', 'zh'), 0, 0, tiled=True)  7.89 us
  transfers between devices with their start and end apart: 3, of which 3 were waited for; matrix products, arithmetic and copies ran while one was open for 0% of the time, Pallas kernels for 0%

profile of v3, /device:TPU:1, one launch (start us, length us, event | category | flops | bytes accessed | tf_op | source)
XLA Modules:
  0.0 185.4 jit_solution(8767587745582772286)
XLA Ops:
  0.6 0.6 pad_add_fusion.place_ref
  1.2 3.5 %pick.1 = f32[32,8,128]{2,1,0:T(8,128)} custom-call(s32[2]{0:T(128)} %pad_add_fusion.place_ref, s32[1,512]{1,0:T(1,128)} %bitcast.13, f32[256,1280]{1,0:T(8,128)} %emb_ref.1, f32[256,512]{1,0:T(8,128)} %fac_ref.1), custom_call_target="tpu_custom_call" | custom-call | tf_op jit(solution)/shard_map/pick/pallas_call | solution.py:276
  4.8 18.0 %all_to_all.30 = f32[32,8,128]{2,1,0:T(8,128)S(1)} all-to-all(f32[32,8,128]{2,1,0:T(8,128)} %pick.1), channel_id=1, replica_groups=mesh['zl'=8,'core'=2,'zh'=2,'x'=4,'y'=4] {'core','x','y'}, dimensions={0} | all-to-all | bytes 262144 | tf_op jit(solution)/shard_map/all_to_all | solution.py:290
  22.9 34.2 %all_to_all.31 = f32[16,48,128]{2,1,0:T(8,128)S(1)} all-to-all(f32[16,48,128]{2,1,0:T(8,128)S(1)} %broadcast_in_dim.9), channel_id=1, replica_groups=mesh['zl'=8,'core'=2,'zh'=2,'x'=4,'y'=4] {'zl','zh'}, dimensions={0} | all-to-all | bytes 786432 | tf_op jit(solution)/shard_map/all_to_all | solution.py:293
  57.1 0.9 select.1
  58.0 0.2 broadcast_in_dim.10
  58.3 0.0 copy-start
  58.3 25.4 %all_to_all.32 = f32[16,56,512]{2,1,0:T(8,128)S(1)} all-to-all(f32[16,56,512]{2,1,0:T(8,128)S(1)} %broadcast_in_dim.10), channel_id=1, replica_groups=mesh['zl'=8,'core'=2,'zh'=2,'x'=4,'y'=4] {'x','y'}, dimensions={0} | all-to-all | bytes 3670016 | tf_op jit(solution)/shard_map/all_to_all | solution.py:303
  83.7 6.7 %collective-permute-start = (f32[896,512]{1,0:T(8,128)S(1)}, f32[896,512]{1,0:T(8,128)S(1)}, u32[]{:S(2)}, u32[]{:S(2)}) collective-permute-start(f32[896,512]{1,0:T(8,128)S(1)} %bitcast.9), channel_id=1, source_target_pairs={{0,32},{32,0},{1,33},{33,1},{2,34},{34,2},{3,35},{35,3},{4,36},{36... | collective-permute-start | bytes 5505032 | tf_op jit(solution)/shard_map/ppermute | solution.py:304
  90.4 3.2 %collective-permute-done.other_ref = f32[896,512]{1,0:T(8,128)S(1)} collective-permute-done((f32[896,512]{1,0:T(8,128)S(1)}, f32[896,512]{1,0:T(8,128)S(1)}, u32[]{:S(2)}, u32[]{:S(2)}) %collective-permute-start) | collective-permute-done | bytes 1835040 | tf_op jit(solution)/shard_map/ppermute | solution.py:304
  93.6 28.1 %main.1 = (f32[256,512]{1,0:T(8,128)}, f32[16,2,16,512]{3,2,1,0:T(8,128)S(1)}, f32[16,2,16,512]{3,2,1,0:T(8,128)S(1)}) custom-call(s32[2]{0:T(128)S(1)} %copy-done.2, f32[256,1280]{1,0:T(8,128)S(1)} %copy-done, f32[256,512]{1,0:T(8,128)S(1)} %copy-done.1, f32[896,512]{1,0:T(8,128)S(1)} %bitcast.10, f32[896,512]{1,0:T(8,128)S(1)} %collective-permute-done.other_ref), custom_call_target="tpu_custom_call" | custom-call | tf_op jit(solution)/shard_map/main/pallas_call | solution.py:308
  121.7 2.3 %collective-permute-start.1 = (f32[16,2,16,512]{3,2,1,0:T(8,128)S(1)}, f32[16,2,16,512]{3,2,1,0:T(8,128)S(1)}, u32[]{:S(2)}, u32[]{:S(2)}) collective-permute-start(f32[16,2,16,512]{3,2,1,0:T(8,128)S(1)} %get-tuple-element.7), channel_id=1, source_target_pairs={{0,32},{32,0},{1,33},{33,1},{2,34},{34,2},{3,35},{35,3},{4,36},{36... | collective-permute-start | bytes 3145736 | tf_op jit(solution)/shard_map/ppermute | solution.py:326
  124.0 2.3 %collective-permute-done.1 = f32[16,2,16,512]{3,2,1,0:T(8,128)S(1)} collective-permute-done((f32[16,2,16,512]{3,2,1,0:T(8,128)S(1)}, f32[16,2,16,512]{3,2,1,0:T(8,128)S(1)}, u32[]{:S(2)}, u32[]{:S(2)}) %collective-permute-start.1) | collective-permute-done | bytes 1048608 | tf_op jit(solution)/shard_map/ppermute | solution.py:326
  126.3 0.2 add.55
  126.5 19.3 %all_to_all.33 = f32[16,2,16,512]{3,2,1,0:T(8,128)S(1)} all-to-all(f32[16,2,16,512]{3,2,1,0:T(8,128)S(1)} %add.55), channel_id=1, replica_groups=mesh['zl'=8,'core'=2,'zh'=2,'x'=4,'y'=4] {'x','y'}, dimensions={0} | all-to-all | bytes 2097152 | tf_op jit(solution)/shard_map/all_to_all | solution.py:327
  145.7 0.1 reduce_sum.18
  145.8 0.1 copy.6
  145.9 0.7 copy.7
  146.5 7.9 %all-to-all-start.4 = ((f32[16,2,512]{2,1,0:T(2,128)}), f32[16,2,512]{2,1,0:T(2,128)S(1)}, u32[]{:S(2)}, u32[]{:S(2)}) async-start(f32[16,2,512]{2,1,0:T(2,128)} %bitcast.7), calls=%async_computation.4 | async-start | bytes 131072 | tf_op jit(solution)/shard_map/all_to_all | solution.py:331
  154.5 12.1 %all-to-all-done.4 = f32[16,2,512]{2,1,0:T(2,128)S(1)} async-done(((f32[16,2,512]{2,1,0:T(2,128)}), f32[16,2,512]{2,1,0:T(2,128)S(1)}, u32[]{:S(2)}, u32[]{:S(2)}) %all-to-all-start.4) | async-done | bytes 65568 | tf_op jit(solution)/shard_map/all_to_all | solution.py:331
  166.6 0.1 fusion
  166.7 11.9 %all_to_all.34 = f32[8,2,512]{2,1,0:T(2,128)S(1)} all-to-all(f32[8,2,512]{2,1,0:T(2,128)S(1)} %broadcast_in_dim.11), channel_id=1, replica_groups=mesh['zl'=8,'core'=2,'zh'=2,'x'=4,'y'=4] {'zl'}, dimensions={0} | all-to-all | bytes 65536 | tf_op jit(solution)/shard_map/all_to_all | solution.py:337
  178.6 6.3 %all_gather.3 = f32[32,512]{1,0:T(8,128)S(1)} all-gather(f32[16,512]{1,0:T(8,128)S(1)} %reshape.59), channel_id=1, replica_groups=mesh['zl'=8,'core'=2,'zh'=2,'x'=4,'y'=4] {'core'}, dimensions={0}, use_global_device_ids=true | all-gather | bytes 98304 | tf_op jit(solution)/shard_map/all_gather | solution.py:338
  184.8 0.6 copy.9
  (13 shorter events, 0.2 us)
Async XLA Ops:
  58.3 35.3 %copy-start = (f32[256,1280]{1,0:T(8,128)S(1)}, f32[256,1280]{1,0:T(8,128)}, u32[]{:S(2)}) copy-start(f32[256,1280]{1,0:T(8,128)} %emb_ref.1) | copy-start | bytes 3932164
  58.3 35.3 %copy-start.1 = (f32[256,512]{1,0:T(8,128)S(1)}, f32[256,512]{1,0:T(8,128)}, u32[]{:S(2)}) copy-start(f32[256,512]{1,0:T(8,128)} %fac_ref.1) | copy-start | bytes 1572868
  58.3 35.3 %copy-start.2 = (s32[2]{0:T(128)S(1)}, s32[2]{0:T(128)}, u32[]{:S(2)}) copy-start(s32[2]{0:T(128)} %pad_add_fusion.place_ref) | copy-start | bytes 28
  83.7 9.9 %collective-permute-start = (f32[896,512]{1,0:T(8,128)S(1)}, f32[896,512]{1,0:T(8,128)S(1)}, u32[]{:S(2)}, u32[]{:S(2)}) collective-permute-start(f32[896,512]{1,0:T(8,128)S(1)} %bitcast.9), channel_id=1, source_target_pairs={{0,32},{32,0},{1,33},{33,1},{2,34},{34,2},{3,35},{35,3},{4,36},{36... | collective-permute-start | bytes 5505032 | tf_op jit(solution)/shard_map/ppermute | solution.py:304
  121.7 4.5 %collective-permute-start.1 = (f32[16,2,16,512]{3,2,1,0:T(8,128)S(1)}, f32[16,2,16,512]{3,2,1,0:T(8,128)S(1)}, u32[]{:S(2)}, u32[]{:S(2)}) collective-permute-start(f32[16,2,16,512]{3,2,1,0:T(8,128)S(1)} %get-tuple-element.7), channel_id=1, source_target_pairs={{0,32},{32,0},{1,33},{33,1},{2,34},{34,2},{3,35},{35,3},{4,36},{36... | collective-permute-start | bytes 3145736 | tf_op jit(solution)/shard_map/ppermute | solution.py:326
  146.5 20.0 %all-to-all-start.4 = ((f32[16,2,512]{2,1,0:T(2,128)}), f32[16,2,512]{2,1,0:T(2,128)S(1)}, u32[]{:S(2)}, u32[]{:S(2)}) async-start(f32[16,2,512]{2,1,0:T(2,128)} %bitcast.7), calls=%async_computation.4 | async-start | bytes 131072 | tf_op jit(solution)/shard_map/all_to_all | solution.py:331

commit v4 on v3

--- a/solution.py
+++ b/solution.py
@@ -45,7 +45,7 @@
 
 
 def pick_kernel(
-    width, place_ref, pivots_hbm, emb_hbm, fac_hbm, out_ref, pivots_ref, emb_ref, fac_ref, sems
+    width, base_ref, core_ref, pivots_hbm, emb_hbm, fac_hbm, out_ref, pivots_ref, emb_ref, fac_ref, sems
 ):
     copies = [
         pltpu.make_async_copy(src, dst, sems.at[i])
@@ -56,7 +56,7 @@
     for copy in copies:
         copy.start()
     copies[0].wait()
-    base, core = place_ref[0], place_ref[1]
+    base, core = base_ref[0], core_ref[0]
     rows_dev = emb_ref.shape[0]
     count = pivots_ref.shape[1]
     local = (pivots_ref[...] - base).astype(f32)
@@ -77,11 +77,13 @@
         tag = jnp.where((sub_tag == k), jnp.where(valid, pos, -1.0), tag)
         inside = jnp.where(hit, 0.0, inside)
     hot = hot.astype(bf16)
+    copies[1].wait()
+    copies[2].wait()
     pieces = []
-    for ref, copy in ((emb_ref, copies[1]), (fac_ref, copies[2])):
-        copy.wait()
-        for c in range(0, ref.shape[1], 256):
-            high, mid, low = split3(ref[:, c : c + 256])
+    for h in range(2):
+        for ref in (emb_ref, fac_ref):
+            step = ref.shape[1] // 2
+            high, mid, low = split3(ref[:, h * step : (h + 1) * step])
             pieces.append(mul(hot, high, NN) + (mul(hot, mid, NN) + mul(hot, low, NN)))
     rows = jnp.concatenate(pieces + [jnp.zeros((8, BLOCK), f32)], axis=1)
     lane_out = lax.broadcasted_iota(jnp.int32, (8, BLOCK), 1)
@@ -162,35 +164,20 @@
             e_ref[at, :] = e
 
 
-def main_kernel(
-    place_ref, emb_ref, fac_ref, own_ref, other_ref, new_ref, keep_ref, send_ref,
-    ch_ref, cl_ref, sq_ref, mat_ref, inv_ref, d_ref, e_ref, sum_ref,
-):
-    core = place_ref[1]
-    rows_dev, width = emb_ref.shape
-    old_rank = fac_ref.shape[1]
-    half, count = own_ref.shape
-    total = 2 * half
-    second = width - half
-    scale = 1.0 / (2.0 * width)
-
-    def take(ref, which):
-        start = pl.multiple_of(which * half, BLOCK)
-        sq = jnp.zeros((1, count), f32)
-        for r in range(0, half, BLOCK):
-            a = ref[r : r + BLOCK, :]
-            high, low = split2(a)
-            at = pl.ds(pl.multiple_of(start + r, BLOCK), BLOCK)
-            ch_ref[at, :] = high
-            cl_ref[at, :] = low
-            part = jnp.sum(a * a, axis=0, keepdims=True)
-            if r >= second:
-                part = jnp.where(which == 0, part, 0.0)
-            sq = sq + part
-        return sq
-
-    sq = take(own_ref, core) + take(other_ref, 1 - core)
-    sq_ref[...] = jnp.transpose(jnp.broadcast_to(sq, (BLOCK, count)))
+def load_half(src_ref, emb_part, ch_ref, cl_ref):
+    half, count = src_ref.shape
+    sq = jnp.zeros((1, count), f32)
+    for r in range(0, half, BLOCK):
+        a = src_ref[r : r + BLOCK, :]
+        ch_ref[r : r + BLOCK, :], cl_ref[r : r + BLOCK, :] = split2(a)
+        if r < emb_part:
+            sq = sq + jnp.sum(a * a, axis=0, keepdims=True)
+    return sq
+
+
+def products(which, emb_ref, fac_ref, ch_ref, cl_ref, emit):
+    half, count = ch_ref.shape
+    emb_part, fac_part = emb_ref.shape[1] // 2, fac_ref.shape[1] // 2
 
     def wide(lo, hi, need):
         return ch_ref[lo:hi, :need], cl_ref[lo:hi, :need]
@@ -198,22 +185,58 @@
     for i in range(count // BLOCK):
         at = slice(i * BLOCK, (i + 1) * BLOCK)
         need = (i // 2 + 1) * 2 * BLOCK
-        cross = mul3((ch_ref[:width, at], cl_ref[:width, at]), wide(0, width, need), TN)
-        old = mul3((ch_ref[width:, at], cl_ref[width:, at]), wide(width, total, need), TN)
-        left = sq_ref[at, 0:1]
+        cross = mul3((ch_ref[:emb_part, at], cl_ref[:emb_part, at]), wide(0, emb_part, need), TN)
+        old = mul3((ch_ref[emb_part:, at], cl_ref[emb_part:, at]), wide(emb_part, half, need), TN)
+        emit(i * BLOCK, need, cross, old)
+    emb_at = pl.ds(pl.multiple_of(which * emb_part, BLOCK), emb_part)
+    fac_at = pl.ds(pl.multiple_of(which * fac_part, BLOCK), fac_part)
+    for r in range(0, emb_ref.shape[0], BLOCK):
+        cross = mul3(split2(emb_ref[r : r + BLOCK, emb_at]), wide(0, emb_part, count), NN)
+        old = mul3(split2(fac_ref[r : r + BLOCK, fac_at]), wide(emb_part, half, count), NN)
+        emit(count + r, count, cross, old)
+
+
+def first_kernel(core_ref, emb_ref, fac_ref, own_ref, cross_ref, old_ref, sq_ref, ch_ref, cl_ref):
+    sq = load_half(own_ref, emb_ref.shape[1] // 2, ch_ref, cl_ref)
+    sq_ref[...] = jnp.broadcast_to(sq, sq_ref.shape)
+
+    def emit(row, need, cross, old):
+        cross_ref[row : row + BLOCK, :need] = cross
+        old_ref[row : row + BLOCK, :need] = old
+
+    products(core_ref[0], emb_ref, fac_ref, ch_ref, cl_ref, emit)
+
+
+def main_kernel(
+    core_ref, emb_ref, fac_ref, other_ref, cross_ref, old_ref, own_sq_ref,
+    new_ref, keep_ref, send_ref,
+    ch_ref, cl_ref, sq_ref, mat_ref, inv_ref, d_ref, e_ref, sum_ref,
+):
+    core = core_ref[0]
+    rows_dev, width = emb_ref.shape
+    old_rank = fac_ref.shape[1]
+    count = other_ref.shape[1]
+    scale = 1.0 / (2.0 * width)
+    sq = own_sq_ref[0:1, :] + load_half(other_ref, width // 2, ch_ref, cl_ref)
+    sq_ref[...] = jnp.transpose(jnp.broadcast_to(sq, (BLOCK, count)))
+
+    def emit(row, need, cross, old):
+        at = slice(row, row + BLOCK)
+        cross = cross_ref[at, :need] + cross
+        old = old_ref[at, :need] + old
+        if row < count:
+            left = sq_ref[at, 0:1]
+        else:
+            a = emb_ref[row - count : row - count + BLOCK, :]
+            left = jnp.sum(a * a, axis=1, keepdims=True)
         block = jnp.exp((2.0 * cross - (left + sq[:, :need])) * scale) - old
-        row = lax.broadcasted_iota(jnp.int32, (BLOCK, need), 0) + i * BLOCK
-        col = lax.broadcasted_iota(jnp.int32, (BLOCK, need), 1)
-        mat_ref[at, :need] = block + jnp.where(row == col, ridge_term, 0.0)
-    for i in range(rows_dev // BLOCK):
-        at = slice(i * BLOCK, (i + 1) * BLOCK)
-        a = emb_ref[at, :]
-        cross = mul3(split2(a), wide(0, width, count), NN)
-        old = mul3(split2(fac_ref[at, :]), wide(width, total, count), NN)
-        left = jnp.sum(a * a, axis=1, keepdims=True)
-        mat_ref[count + i * BLOCK : count + (i + 1) * BLOCK, :] = (
-            jnp.exp((2.0 * cross - (left + sq)) * scale) - old
-        )
+        if row < count:
+            r = lax.broadcasted_iota(jnp.int32, (BLOCK, need), 0) + row
+            c = lax.broadcasted_iota(jnp.int32, (BLOCK, need), 1)
+            block = block + jnp.where(r == c, ridge_term, 0.0)
+        mat_ref[at, :need] = block
+
+    products(1 - core, emb_ref, fac_ref, ch_ref, cl_ref, emit)
 
     all_rows = count + rows_dev
 
@@ -272,11 +295,12 @@
     piece = total // slices
     core = lax.axis_index("core")
     mine = lax.axis_index(("zl", "core", "zh", "x", "y"))
-    place = jnp.stack([mine * rows_dev, core]).astype(jnp.int32)
+    base_place = (mine * rows_dev).astype(jnp.int32).reshape(1)
+    core_place = core.astype(jnp.int32).reshape(1)
     sent = pl.pallas_call(
         functools.partial(pick_kernel, piece),
         out_shape=jax.ShapeDtypeStruct((slices, 8, BLOCK), f32),
-        in_specs=[SMEM, HBM, HBM, HBM],
+        in_specs=[SMEM, SMEM, HBM, HBM, HBM],
         out_specs=VMEM,
         scratch_shapes=[
             pltpu.VMEM((1, count), jnp.int32),
@@ -286,7 +310,7 @@
         ],
         compiler_params=WIDE_PARAMS,
         name="pick",
-    )(place, pivots.reshape(1, count), embeddings, factor)
+    )(base_place, core_place, pivots.reshape(1, count), embeddings, factor)
     got = lax.all_to_all(sent, ("core", "x", "y"), 0, 0, tiled=True)
     packed = (got[:n_xy] + got[n_xy:])[:, :SLOTS].reshape(n_xy * SLOTS, BLOCK)
     packed = jnp.broadcast_to(packed[None], (n_z, n_xy * SLOTS, BLOCK))
@@ -302,17 +326,31 @@
     wide = jnp.broadcast_to(chosen_slice[None], (n_xy, piece, count))
     own = lax.all_to_all(wide, ("x", "y"), 0, 0, tiled=True).reshape(n_xy * piece, count)
     other = lax.ppermute(own, "core", [(0, 1), (1, 0)])
+    half = total // 2
+    all_rows = count + rows_dev
+    halves = [pltpu.VMEM((half, count), bf16), pltpu.VMEM((half, count), bf16)]
+    table = jax.ShapeDtypeStruct((all_rows, count), f32)
+    cross, old, own_sq = pl.pallas_call(
+        first_kernel,
+        out_shape=(table, table, jax.ShapeDtypeStruct((8, count), f32)),
+        in_specs=[SMEM, VMEM, VMEM, VMEM],
+        out_specs=(VMEM, VMEM, VMEM),
+        scratch_shapes=halves,
+        compiler_params=PARAMS,
+        cost_estimate=pl.CostEstimate(
+            flops=6 * half * count * all_rows, bytes_accessed=4 * half * count, transcendentals=0
+        ),
+        name="first",
+    )(core_place, embeddings, factor, own)
     share = (old_rank + count) // slices
     part = share // 2
     split = jax.ShapeDtypeStruct((n_xy, 2, part, count), f32)
     new_factor, keep, send = pl.pallas_call(
         main_kernel,
         out_shape=(jax.ShapeDtypeStruct((rows_dev, count), f32), split, split),
-        in_specs=[SMEM, VMEM, VMEM, VMEM, VMEM],
+        in_specs=[SMEM] + [VMEM] * 6,
         out_specs=(VMEM, VMEM, VMEM),
-        scratch_shapes=[
-            pltpu.VMEM((total, count), bf16),
-            pltpu.VMEM((total, count), bf16),
+        scratch_shapes=halves + [
             pltpu.VMEM((count, BLOCK), f32),
             pltpu.VMEM((count + rows_dev, count), f32),
             pltpu.VMEM((BLOCK, BLOCK), f32),
@@ -322,7 +360,7 @@
         ],
         compiler_params=PARAMS,
         name="main",
-    )(place, embeddings, factor, own, other)
+    )(core_place, embeddings, factor, other, cross, old, own_sq)
     pair = keep + lax.ppermute(send, "core", [(0, 1), (1, 0)])
     layer = jnp.sum(lax.all_to_all(pair, ("x", "y"), 0, 0, tiled=True), axis=0)
     n_zl = n_z // 2

time: 186 us -> 182 us (0.978)
  waiting for transfers between devices: 17.6 us -> 15.1 us
    pallas_call x1, Pallas kernels: 28.1 us -> 25.2 us  [on_device(): pl.pallas_call(main_kernel, out_shape=(jax.ShapeDtypeStruct((rows_dev, co...]
    ppermute x1, waiting for transfers between devices: 3.21 us -> 0.72 us  [on_device(): other = lax.ppermute(own, 'core', [(0, 1), (1, 0)])]
    pallas_call x0 -> x1, Pallas kernels: none -> 2.46 us  [on_device(): pl.pallas_call(first_kernel, out_shape=(table, table, jax.ShapeDtypeStruc...]
  transfers between devices with their start and end apart: 3 -> 3, of which waited for: 3 -> 3; matrix products, arithmetic and copies ran while one was open for 0% -> 0% of each run, Pallas kernels for 0% -> 1%
where the time goes in v4:
time: 182 us; the launch traced here: 181 us
  blocking collectives  115 us (63%)
  Pallas kernels  31.4 us (17%)
  starting transfers between devices  16.9 us (9%)
  waiting for transfers between devices  15.1 us (8%)
    all_to_all x1, blocking collectives, on_device(): slots = lax.all_to_all(packed, ('zl', 'zh'), 0, 0, tiled=True)  34.2 us
    all_to_all x1, blocking collectives, on_device(): lax.all_to_all(wide, ('x', 'y'), 0, 0, tiled=True)  25.4 us
    pallas_call x1, Pallas kernels, on_device(): pl.pallas_call(main_kernel, out_shape=(jax.ShapeDtypeStruct((rows_dev, co...  25.2 us
    all_to_all x1, blocking collectives, on_device(): layer = jnp.sum(lax.all_to_all(pair, ('x', 'y'), 0, 0, tiled=True), axis=0)  19.3 us
    all_to_all x1, blocking collectives, on_device(): got = lax.all_to_all(sent, ('core', 'x', 'y'), 0, 0, tiled=True)  18 us
    all_to_all x1, waiting for transfers between devices, on_device(): lax.all_to_all(spread, ('zl', 'zh'), 0, 0, tiled=True)  12.1 us
    all_to_all x1, blocking collectives, on_device(): line = lax.all_to_all(line, 'zl', 0, 0, tiled=True).reshape(part, count)  11.9 us
    all_to_all x1, starting transfers between devices, on_device(): lax.all_to_all(spread, ('zl', 'zh'), 0, 0, tiled=True)  7.89 us
  transfers between devices with their start and end apart: 3, of which 3 were waited for; matrix products, arithmetic and copies ran while one was open for 0% of the time, Pallas kernels for 1%

profile of v4, /device:TPU:1, one launch (start us, length us, event | category | flops | bytes accessed | tf_op | source)
XLA Modules:
  0.0 181.2 jit_solution(12838720761509638795)
XLA Ops:
  0.6 2.8 %pick.1 = f32[32,8,128]{2,1,0:T(8,128)} custom-call(s32[1]{0:T(128)} %bitcast.1.base_ref, s32[1]{0:T(128)} %bitcast.core_ref, s32[1,512]{1,0:T(1,128)} %bitcast.13, f32[256,1280]{1,0:T(8,128)} %emb_ref.3, f32[256,512]{1,0:T(8,128)} %fac_ref.3), custom_call_target="tpu_custom_call" | custom-call | tf_op jit(solution)/shard_map/pick/pallas_call | solution.py:300
  3.5 18.0 %all_to_all.30 = f32[32,8,128]{2,1,0:T(8,128)S(1)} all-to-all(f32[32,8,128]{2,1,0:T(8,128)} %pick.1), channel_id=1, replica_groups=mesh['zl'=8,'core'=2,'zh'=2,'x'=4,'y'=4] {'core','x','y'}, dimensions={0} | all-to-all | bytes 262144 | tf_op jit(solution)/shard_map/all_to_all | solution.py:314
  21.6 34.2 %all_to_all.31 = f32[16,48,128]{2,1,0:T(8,128)S(1)} all-to-all(f32[16,48,128]{2,1,0:T(8,128)S(1)} %broadcast_in_dim.9), channel_id=1, replica_groups=mesh['zl'=8,'core'=2,'zh'=2,'x'=4,'y'=4] {'zl','zh'}, dimensions={0} | all-to-all | bytes 786432 | tf_op jit(solution)/shard_map/all_to_all | solution.py:317
  55.8 0.9 select.1
  56.7 0.2 broadcast_in_dim.10
  56.9 0.0 copy-start
  57.0 25.4 %all_to_all.32 = f32[16,56,512]{2,1,0:T(8,128)S(1)} all-to-all(f32[16,56,512]{2,1,0:T(8,128)S(1)} %broadcast_in_dim.10), channel_id=1, replica_groups=mesh['zl'=8,'core'=2,'zh'=2,'x'=4,'y'=4] {'x','y'}, dimensions={0} | all-to-all | bytes 3670016 | tf_op jit(solution)/shard_map/all_to_all | solution.py:327
  82.3 6.7 %collective-permute-start = (f32[896,512]{1,0:T(8,128)S(1)}, f32[896,512]{1,0:T(8,128)S(1)}, u32[]{:S(2)}, u32[]{:S(2)}) collective-permute-start(f32[896,512]{1,0:T(8,128)S(1)} %bitcast.9), channel_id=1, source_target_pairs={{0,32},{32,0},{1,33},{33,1},{2,34},{34,2},{3,35},{35,3},{4,36},{36... | collective-permute-start | bytes 5505032 | tf_op jit(solution)/shard_map/ppermute | solution.py:328
  89.1 2.5 %first.1 = (f32[768,512]{1,0:T(8,128)S(1)}, f32[768,512]{1,0:T(8,128)S(1)}, f32[8,512]{1,0:T(8,128)S(1)}) custom-call(s32[1]{0:T(128)} %bitcast.core_ref, f32[256,1280]{1,0:T(8,128)S(1)} %copy-done, f32[256,512]{1,0:T(8,128)S(1)} %copy-done.1, f32[896,512]{1,0:T(8,128)S(1)} %bitcast.10), custom_call_target="tpu_custom_call" | custom-call | flops 2113929216 | bytes 1835008 | tf_op jit(solution)/shard_map/first/pallas_call | solution.py:333
  91.6 0.7 collective-permute-done.other_ref
  92.3 25.2 %main.1 = (f32[256,512]{1,0:T(8,128)}, f32[16,2,16,512]{3,2,1,0:T(8,128)S(1)}, f32[16,2,16,512]{3,2,1,0:T(8,128)S(1)}) custom-call(s32[1]{0:T(128)} %bitcast.core_ref, f32[256,1280]{1,0:T(8,128)S(1)} %copy-done, f32[256,512]{1,0:T(8,128)S(1)} %copy-done.1, f32[896,512]{1,0:T(8,128)S(1)} %collective-permute-done.other_ref, ...), custom_call_target="tpu_custom_call" | custom-call | tf_op jit(solution)/shard_map/main/pallas_call | solution.py:348
  117.4 2.3 %collective-permute-start.1 = (f32[16,2,16,512]{3,2,1,0:T(8,128)S(1)}, f32[16,2,16,512]{3,2,1,0:T(8,128)S(1)}, u32[]{:S(2)}, u32[]{:S(2)}) collective-permute-start(f32[16,2,16,512]{3,2,1,0:T(8,128)S(1)} %get-tuple-element.13), channel_id=1, source_target_pairs={{0,32},{32,0},{1,33},{33,1},{2,34},{34,2},{3,35},{35,3},{4,36},{36... | collective-permute-start | bytes 3145736 | tf_op jit(solution)/shard_map/ppermute | solution.py:364
  119.8 2.3 %collective-permute-done.1 = f32[16,2,16,512]{3,2,1,0:T(8,128)S(1)} collective-permute-done((f32[16,2,16,512]{3,2,1,0:T(8,128)S(1)}, f32[16,2,16,512]{3,2,1,0:T(8,128)S(1)}, u32[]{:S(2)}, u32[]{:S(2)}) %collective-permute-start.1) | collective-permute-done | bytes 1048608 | tf_op jit(solution)/shard_map/ppermute | solution.py:364
  122.0 0.2 add.55
  122.2 19.3 %all_to_all.33 = f32[16,2,16,512]{3,2,1,0:T(8,128)S(1)} all-to-all(f32[16,2,16,512]{3,2,1,0:T(8,128)S(1)} %add.55), channel_id=1, replica_groups=mesh['zl'=8,'core'=2,'zh'=2,'x'=4,'y'=4] {'x','y'}, dimensions={0} | all-to-all | bytes 2097152 | tf_op jit(solution)/shard_map/all_to_all | solution.py:365
  141.5 0.1 reduce_sum.18
  141.6 0.1 copy.6
  141.6 0.7 copy.7
  142.3 7.9 %all-to-all-start.4 = ((f32[16,2,512]{2,1,0:T(2,128)}), f32[16,2,512]{2,1,0:T(2,128)S(1)}, u32[]{:S(2)}, u32[]{:S(2)}) async-start(f32[16,2,512]{2,1,0:T(2,128)} %bitcast.7), calls=%async_computation.4 | async-start | bytes 131072 | tf_op jit(solution)/shard_map/all_to_all | solution.py:369
  150.2 12.1 %all-to-all-done.4 = f32[16,2,512]{2,1,0:T(2,128)S(1)} async-done(((f32[16,2,512]{2,1,0:T(2,128)}), f32[16,2,512]{2,1,0:T(2,128)S(1)}, u32[]{:S(2)}, u32[]{:S(2)}) %all-to-all-start.4) | async-done | bytes 65568 | tf_op jit(solution)/shard_map/all_to_all | solution.py:369
  162.3 0.1 fusion
  162.4 11.9 %all_to_all.34 = f32[8,2,512]{2,1,0:T(2,128)S(1)} all-to-all(f32[8,2,512]{2,1,0:T(2,128)S(1)} %broadcast_in_dim.11), channel_id=1, replica_groups=mesh['zl'=8,'core'=2,'zh'=2,'x'=4,'y'=4] {'zl'}, dimensions={0} | all-to-all | bytes 65536 | tf_op jit(solution)/shard_map/all_to_all | solution.py:375
  174.3 6.3 %all_gather.3 = f32[32,512]{1,0:T(8,128)S(1)} all-gather(f32[16,512]{1,0:T(8,128)S(1)} %reshape.67), channel_id=1, replica_groups=mesh['zl'=8,'core'=2,'zh'=2,'x'=4,'y'=4] {'core'}, dimensions={0}, use_global_device_ids=true | all-gather | bytes 98304 | tf_op jit(solution)/shard_map/all_gather | solution.py:376
  180.6 0.6 copy.9
  (11 shorter events, 0.1 us)
Async XLA Ops:
  56.9 32.1 %copy-start = (f32[256,1280]{1,0:T(8,128)S(1)}, f32[256,1280]{1,0:T(8,128)}, u32[]{:S(2)}) copy-start(f32[256,1280]{1,0:T(8,128)} %emb_ref.3) | copy-start | bytes 3932164
  57.0 32.1 %copy-start.1 = (f32[256,512]{1,0:T(8,128)S(1)}, f32[256,512]{1,0:T(8,128)}, u32[]{:S(2)}) copy-start(f32[256,512]{1,0:T(8,128)} %fac_ref.3) | copy-start | bytes 1572868
  82.3 9.9 %collective-permute-start = (f32[896,512]{1,0:T(8,128)S(1)}, f32[896,512]{1,0:T(8,128)S(1)}, u32[]{:S(2)}, u32[]{:S(2)}) collective-permute-start(f32[896,512]{1,0:T(8,128)S(1)} %bitcast.9), channel_id=1, source_target_pairs={{0,32},{32,0},{1,33},{33,1},{2,34},{34,2},{3,35},{35,3},{4,36},{36... | collective-permute-start | bytes 5505032 | tf_op jit(solution)/shard_map/ppermute | solution.py:328
  117.4 4.6 %collective-permute-start.1 = (f32[16,2,16,512]{3,2,1,0:T(8,128)S(1)}, f32[16,2,16,512]{3,2,1,0:T(8,128)S(1)}, u32[]{:S(2)}, u32[]{:S(2)}) collective-permute-start(f32[16,2,16,512]{3,2,1,0:T(8,128)S(1)} %get-tuple-element.13), channel_id=1, source_target_pairs={{0,32},{32,0},{1,33},{33,1},{2,34},{34,2},{3,35},{35,3},{4,36},{36... | collective-permute-start | bytes 3145736 | tf_op jit(solution)/shard_map/ppermute | solution.py:364
  142.3 20.0 %all-to-all-start.4 = ((f32[16,2,512]{2,1,0:T(2,128)}), f32[16,2,512]{2,1,0:T(2,128)S(1)}, u32[]{:S(2)}, u32[]{:S(2)}) async-start(f32[16,2,512]{2,1,0:T(2,128)} %bitcast.7), calls=%async_computation.4 | async-start | bytes 131072 | tf_op jit(solution)/shard_map/all_to_all | solution.py:369

commit v5 on v4

--- a/solution.py
+++ b/solution.py
@@ -95,7 +95,7 @@
             window = pltpu.roll(window, 2 * BLOCK - (first - tile), 1)
         piece = jnp.where(lane_out < width, window[:, :BLOCK], jnp.where(lane_out == width, tag, 0.0))
         piece = jnp.where(core == 0, piece, pltpu.roll(piece, BLOCK // 2, 1))
-        out_ref[j] = piece
+        out_ref[j] = piece[:4]
 
 
 def select_kernel(width, slots_ref, out_ref):
@@ -114,7 +114,7 @@
     out_ref[...] = total
 
 
-def factor_block(mat_ref, off, inv_ref, d_ref, e_ref):
+def factor_block(mat_ref, off, inv_ref, d_ref, e_ref, head_ref):
     d_ref[...] = mat_ref[pl.ds(off, BLOCK), pl.ds(off, BLOCK)]
     e_ref[...] = jnp.where(
         lax.broadcasted_iota(jnp.int32, (BLOCK, BLOCK), 0)
@@ -131,7 +131,16 @@
         first = p * PANEL
         rows = [jnp.broadcast_to(d_ref[first + k : first + k + 1, :], full) for k in range(PANEL)]
         invs = [jnp.broadcast_to(e_ref[first + k : first + k + 1, :], full) for k in range(PANEL)]
-        s = [[spread(rows[i], first + k) for k in range(i + 1)] for i in range(PANEL)]
+        lead = d_ref[first : first + PANEL, :]
+        for k in range(PANEL):
+            head_ref[k * PANEL : (k + 1) * PANEL, :] = spread(lead, first + k)
+        s = [
+            [
+                jnp.broadcast_to(head_ref[k * PANEL + i : k * PANEL + i + 1, :], full)
+                for k in range(i + 1)
+            ]
+            for i in range(PANEL)
+        ]
         scale = []
         for k in range(PANEL):
             r = lax.rsqrt(s[k][k])
@@ -210,7 +219,7 @@
 def main_kernel(
     core_ref, emb_ref, fac_ref, other_ref, cross_ref, old_ref, own_sq_ref,
     new_ref, keep_ref, send_ref,
-    ch_ref, cl_ref, sq_ref, mat_ref, inv_ref, d_ref, e_ref, sum_ref,
+    ch_ref, cl_ref, sq_ref, mat_ref, inv_ref, d_ref, e_ref, head_ref, sum_ref,
 ):
     core = core_ref[0]
     rows_dev, width = emb_ref.shape
@@ -242,7 +251,7 @@
 
     def step(kb, carry):
         off = pl.multiple_of(kb * BLOCK, BLOCK)
-        factor_block(mat_ref, off, inv_ref, d_ref, e_ref)
+        factor_block(mat_ref, off, inv_ref, d_ref, e_ref, head_ref)
         panel = mul3(split2(mat_ref[:, pl.ds(off, BLOCK)]), split2(inv_ref[...]), NT)
         new_ref[:, pl.ds(off, BLOCK)] = panel[count:]
         row = lax.broadcasted_iota(jnp.int32, (all_rows, BLOCK), 0)
@@ -299,7 +308,7 @@
     core_place = core.astype(jnp.int32).reshape(1)
     sent = pl.pallas_call(
         functools.partial(pick_kernel, piece),
-        out_shape=jax.ShapeDtypeStruct((slices, 8, BLOCK), f32),
+        out_shape=jax.ShapeDtypeStruct((slices, 4, BLOCK), f32),
         in_specs=[SMEM, SMEM, HBM, HBM, HBM],
         out_specs=VMEM,
         scratch_shapes=[
@@ -356,6 +365,7 @@
             pltpu.VMEM((BLOCK, BLOCK), f32),
             pltpu.VMEM((BLOCK, BLOCK), f32),
             pltpu.VMEM((BLOCK, BLOCK), f32),
+            pltpu.VMEM((PANEL * PANEL, BLOCK), f32),
             pltpu.VMEM((old_rank + count, count), f32),
         ],
         compiler_params=PARAMS,

time: 182 us -> 178 us (0.978)
  Pallas kernels: 31.4 us -> 28.3 us
    pallas_call x1, Pallas kernels: 25.2 us -> 22.1 us  [on_device(): pl.pallas_call(main_kernel, out_shape=(jax.ShapeDtypeStruct((rows_dev, co...]
where the time goes in v5:
time: 178 us
  blocking collectives  115 us (65%)
  Pallas kernels  28.3 us (16%)
  starting transfers between devices  16.9 us (9%)
  waiting for transfers between devices  15.1 us (8%)
    all_to_all x1, blocking collectives, on_device(): slots = lax.all_to_all(packed, ('zl', 'zh'), 0, 0, tiled=True)  34.4 us
    all_to_all x1, blocking collectives, on_device(): lax.all_to_all(wide, ('x', 'y'), 0, 0, tiled=True)  25.2 us
    pallas_call x1, Pallas kernels, on_device(): pl.pallas_call(main_kernel, out_shape=(jax.ShapeDtypeStruct((rows_dev, co...  22.1 us
    all_to_all x1, blocking collectives, on_device(): layer = jnp.sum(lax.all_to_all(pair, ('x', 'y'), 0, 0, tiled=True), axis=0)  19.3 us
    all_to_all x1, blocking collectives, on_device(): got = lax.all_to_all(sent, ('core', 'x', 'y'), 0, 0, tiled=True)  17.6 us
    all_to_all x1, waiting for transfers between devices, on_device(): lax.all_to_all(spread, ('zl', 'zh'), 0, 0, tiled=True)  12.1 us
    all_to_all x1, blocking collectives, on_device(): line = lax.all_to_all(line, 'zl', 0, 0, tiled=True).reshape(part, count)  11.9 us
    all_to_all x1, starting transfers between devices, on_device(): lax.all_to_all(spread, ('zl', 'zh'), 0, 0, tiled=True)  7.89 us
  transfers between devices with their start and end apart: 3, of which 3 were waited for; matrix products, arithmetic and copies ran while one was open for 0% of the time, Pallas kernels for 1%

profile of v5, /device:TPU:1, one launch (start us, length us, event | category | flops | bytes accessed | tf_op | source)
XLA Modules:
  0.0 177.7 jit_solution(3937079172650214099)
XLA Ops:
  0.6 2.8 %pick.1 = f32[32,4,128]{2,1,0:T(4,128)} custom-call(s32[1]{0:T(128)} %bitcast.1.base_ref, s32[1]{0:T(128)} %bitcast.core_ref, s32[1,512]{1,0:T(1,128)} %bitcast.13, f32[256,1280]{1,0:T(8,128)} %emb_ref.3, f32[256,512]{1,0:T(8,128)} %fac_ref.3), custom_call_target="tpu_custom_call" | custom-call | tf_op jit(solution)/shard_map/pick/pallas_call | solution.py:309
  3.5 17.6 %all_to_all.30 = f32[32,4,128]{2,1,0:T(4,128)S(1)} all-to-all(f32[32,4,128]{2,1,0:T(4,128)} %pick.1), channel_id=1, replica_groups=mesh['zl'=8,'core'=2,'zh'=2,'x'=4,'y'=4] {'core','x','y'}, dimensions={0} | all-to-all | bytes 131072 | tf_op jit(solution)/shard_map/all_to_all | solution.py:323
  21.1 34.4 %all_to_all.31 = f32[16,48,128]{2,1,0:T(8,128)S(1)} all-to-all(f32[16,48,128]{2,1,0:T(8,128)S(1)} %broadcast_in_dim.9), channel_id=1, replica_groups=mesh['zl'=8,'core'=2,'zh'=2,'x'=4,'y'=4] {'zl','zh'}, dimensions={0} | all-to-all | bytes 786432 | tf_op jit(solution)/shard_map/all_to_all | solution.py:326
  55.5 0.9 select.1
  56.4 0.2 broadcast_in_dim.10
  56.7 0.0 copy-start
  56.7 25.2 %all_to_all.32 = f32[16,56,512]{2,1,0:T(8,128)S(1)} all-to-all(f32[16,56,512]{2,1,0:T(8,128)S(1)} %broadcast_in_dim.10), channel_id=1, replica_groups=mesh['zl'=8,'core'=2,'zh'=2,'x'=4,'y'=4] {'x','y'}, dimensions={0} | all-to-all | bytes 3670016 | tf_op jit(solution)/shard_map/all_to_all | solution.py:336
  81.9 6.7 %collective-permute-start = (f32[896,512]{1,0:T(8,128)S(1)}, f32[896,512]{1,0:T(8,128)S(1)}, u32[]{:S(2)}, u32[]{:S(2)}) collective-permute-start(f32[896,512]{1,0:T(8,128)S(1)} %bitcast.9), channel_id=1, source_target_pairs={{0,32},{32,0},{1,33},{33,1},{2,34},{34,2},{3,35},{35,3},{4,36},{36... | collective-permute-start | bytes 5505032 | tf_op jit(solution)/shard_map/ppermute | solution.py:337
  88.6 2.5 %first.1 = (f32[768,512]{1,0:T(8,128)S(1)}, f32[768,512]{1,0:T(8,128)S(1)}, f32[8,512]{1,0:T(8,128)S(1)}) custom-call(s32[1]{0:T(128)} %bitcast.core_ref, f32[256,1280]{1,0:T(8,128)S(1)} %copy-done, f32[256,512]{1,0:T(8,128)S(1)} %copy-done.1, f32[896,512]{1,0:T(8,128)S(1)} %bitcast.10), custom_call_target="tpu_custom_call" | custom-call | flops 2113929216 | bytes 1835008 | tf_op jit(solution)/shard_map/first/pallas_call | solution.py:342
  91.1 0.7 collective-permute-done.other_ref
  91.8 22.1 %main.1 = (f32[256,512]{1,0:T(8,128)}, f32[16,2,16,512]{3,2,1,0:T(8,128)S(1)}, f32[16,2,16,512]{3,2,1,0:T(8,128)S(1)}) custom-call(s32[1]{0:T(128)} %bitcast.core_ref, f32[256,1280]{1,0:T(8,128)S(1)} %copy-done, f32[256,512]{1,0:T(8,128)S(1)} %copy-done.1, f32[896,512]{1,0:T(8,128)S(1)} %collective-permute-done.other_ref, ...), custom_call_target="tpu_custom_call" | custom-call | tf_op jit(solution)/shard_map/main/pallas_call | solution.py:357
  113.9 2.3 %collective-permute-start.1 = (f32[16,2,16,512]{3,2,1,0:T(8,128)S(1)}, f32[16,2,16,512]{3,2,1,0:T(8,128)S(1)}, u32[]{:S(2)}, u32[]{:S(2)}) collective-permute-start(f32[16,2,16,512]{3,2,1,0:T(8,128)S(1)} %get-tuple-element.13), channel_id=1, source_target_pairs={{0,32},{32,0},{1,33},{33,1},{2,34},{34,2},{3,35},{35,3},{4,36},{36... | collective-permute-start | bytes 3145736 | tf_op jit(solution)/shard_map/ppermute | solution.py:374
  116.2 2.3 %collective-permute-done.1 = f32[16,2,16,512]{3,2,1,0:T(8,128)S(1)} collective-permute-done((f32[16,2,16,512]{3,2,1,0:T(8,128)S(1)}, f32[16,2,16,512]{3,2,1,0:T(8,128)S(1)}, u32[]{:S(2)}, u32[]{:S(2)}) %collective-permute-start.1) | collective-permute-done | bytes 1048608 | tf_op jit(solution)/shard_map/ppermute | solution.py:374
  118.5 0.2 add.55
  118.7 19.3 %all_to_all.33 = f32[16,2,16,512]{3,2,1,0:T(8,128)S(1)} all-to-all(f32[16,2,16,512]{3,2,1,0:T(8,128)S(1)} %add.55), channel_id=1, replica_groups=mesh['zl'=8,'core'=2,'zh'=2,'x'=4,'y'=4] {'x','y'}, dimensions={0} | all-to-all | bytes 2097152 | tf_op jit(solution)/shard_map/all_to_all | solution.py:375
  138.0 0.1 reduce_sum.18
  138.0 0.1 copy.6
  138.1 0.7 copy.7
  138.8 7.9 %all-to-all-start.4 = ((f32[16,2,512]{2,1,0:T(2,128)}), f32[16,2,512]{2,1,0:T(2,128)S(1)}, u32[]{:S(2)}, u32[]{:S(2)}) async-start(f32[16,2,512]{2,1,0:T(2,128)} %bitcast.7), calls=%async_computation.4 | async-start | bytes 131072 | tf_op jit(solution)/shard_map/all_to_all | solution.py:379
  146.7 12.1 %all-to-all-done.4 = f32[16,2,512]{2,1,0:T(2,128)S(1)} async-done(((f32[16,2,512]{2,1,0:T(2,128)}), f32[16,2,512]{2,1,0:T(2,128)S(1)}, u32[]{:S(2)}, u32[]{:S(2)}) %all-to-all-start.4) | async-done | bytes 65568 | tf_op jit(solution)/shard_map/all_to_all | solution.py:379
  158.8 0.1 fusion
  158.9 11.9 %all_to_all.34 = f32[8,2,512]{2,1,0:T(2,128)S(1)} all-to-all(f32[8,2,512]{2,1,0:T(2,128)S(1)} %broadcast_in_dim.11), channel_id=1, replica_groups=mesh['zl'=8,'core'=2,'zh'=2,'x'=4,'y'=4] {'zl'}, dimensions={0} | all-to-all | bytes 65536 | tf_op jit(solution)/shard_map/all_to_all | solution.py:385
  170.8 6.3 %all_gather.3 = f32[32,512]{1,0:T(8,128)S(1)} all-gather(f32[16,512]{1,0:T(8,128)S(1)} %reshape.67), channel_id=1, replica_groups=mesh['zl'=8,'core'=2,'zh'=2,'x'=4,'y'=4] {'core'}, dimensions={0}, use_global_device_ids=true | all-gather | bytes 98304 | tf_op jit(solution)/shard_map/all_gather | solution.py:386
  177.0 0.6 copy.9
  (11 shorter events, 0.1 us)
Async XLA Ops:
  56.7 31.9 %copy-start = (f32[256,1280]{1,0:T(8,128)S(1)}, f32[256,1280]{1,0:T(8,128)}, u32[]{:S(2)}) copy-start(f32[256,1280]{1,0:T(8,128)} %emb_ref.3) | copy-start | bytes 3932164
  56.7 31.9 %copy-start.1 = (f32[256,512]{1,0:T(8,128)S(1)}, f32[256,512]{1,0:T(8,128)}, u32[]{:S(2)}) copy-start(f32[256,512]{1,0:T(8,128)} %fac_ref.3) | copy-start | bytes 1572868
  81.9 9.9 %collective-permute-start = (f32[896,512]{1,0:T(8,128)S(1)}, f32[896,512]{1,0:T(8,128)S(1)}, u32[]{:S(2)}, u32[]{:S(2)}) collective-permute-start(f32[896,512]{1,0:T(8,128)S(1)} %bitcast.9), channel_id=1, source_target_pairs={{0,32},{32,0},{1,33},{33,1},{2,34},{34,2},{3,35},{35,3},{4,36},{36... | collective-permute-start | bytes 5505032 | tf_op jit(solution)/shard_map/ppermute | solution.py:337
  113.9 4.6 %collective-permute-start.1 = (f32[16,2,16,512]{3,2,1,0:T(8,128)S(1)}, f32[16,2,16,512]{3,2,1,0:T(8,128)S(1)}, u32[]{:S(2)}, u32[]{:S(2)}) collective-permute-start(f32[16,2,16,512]{3,2,1,0:T(8,128)S(1)} %get-tuple-element.13), channel_id=1, source_target_pairs={{0,32},{32,0},{1,33},{33,1},{2,34},{34,2},{3,35},{35,3},{4,36},{36... | collective-permute-start | bytes 3145736 | tf_op jit(solution)/shard_map/ppermute | solution.py:374
  138.8 20.0 %all-to-all-start.4 = ((f32[16,2,512]{2,1,0:T(2,128)}), f32[16,2,512]{2,1,0:T(2,128)S(1)}, u32[]{:S(2)}, u32[]{:S(2)}) async-start(f32[16,2,512]{2,1,0:T(2,128)} %bitcast.7), calls=%async_computation.4 | async-start | bytes 131072 | tf_op jit(solution)/shard_map/all_to_all | solution.py:379

commit v6 on v5

--- a/solution.py
+++ b/solution.py
@@ -252,18 +252,22 @@
     def step(kb, carry):
         off = pl.multiple_of(kb * BLOCK, BLOCK)
         factor_block(mat_ref, off, inv_ref, d_ref, e_ref, head_ref)
-        panel = mul3(split2(mat_ref[:, pl.ds(off, BLOCK)]), split2(inv_ref[...]), NT)
+        ah, al = split2(mat_ref[:, pl.ds(off, BLOCK)])
+        bh, bl = split2(inv_ref[...])
+        panel = mul(jnp.concatenate([ah, ah, al], axis=1), jnp.concatenate([bh, bl, bh], axis=1), NT)
         new_ref[:, pl.ds(off, BLOCK)] = panel[count:]
         row = lax.broadcasted_iota(jnp.int32, (all_rows, BLOCK), 0)
         panel = jnp.where(row >= off + BLOCK, panel, 0.0)
         high, low = split2(panel)
+        left = jnp.concatenate([high, high, low], axis=1)
+        right = jnp.concatenate([high[:count], low[:count], high[:count]], axis=1)
         for r in range(0, all_rows, 256):
             for c in range(0, min(r + 256, count), 256):
 
                 @pl.when(off + BLOCK < min(r, c) + 256)
                 def _():
-                    mat_ref[r : r + 256, c : c + 256] = mat_ref[r : r + 256, c : c + 256] - mul3(
-                        (high[r : r + 256], low[r : r + 256]), (high[c : c + 256], low[c : c + 256]), NT
+                    mat_ref[r : r + 256, c : c + 256] = mat_ref[r : r + 256, c : c + 256] - mul(
+                        left[r : r + 256], right[c : c + 256], NT
                     )
 
         return carry
@@ -286,6 +290,15 @@
             start = (zh * shares + j) * 2 * part
             keep_ref[j, zh] = sum_ref[pl.ds(pl.multiple_of(start + core * part, part), part), :]
             send_ref[j, zh] = sum_ref[pl.ds(pl.multiple_of(start + (1 - core) * part, part), part), :]
+
+
+def layer_kernel(parts_ref, out_ref):
+    few = out_ref.shape[1]
+    n_zh = parts_ref.shape[1]
+    for zh in range(n_zh):
+        total = jnp.sum(parts_ref[:, zh], axis=0)
+        for zl in range(out_ref.shape[0] // n_zh):
+            out_ref[zl * n_zh + zh] = total[zl * few : (zl + 1) * few]
 
 
 VMEM = pl.BlockSpec(memory_space=pltpu.VMEM)
@@ -372,10 +385,17 @@
         name="main",
     )(core_place, embeddings, factor, other, cross, old, own_sq)
     pair = keep + lax.ppermute(send, "core", [(0, 1), (1, 0)])
-    layer = jnp.sum(lax.all_to_all(pair, ("x", "y"), 0, 0, tiled=True), axis=0)
+    parts = lax.all_to_all(pair, ("x", "y"), 0, 0, tiled=True)
     n_zl = n_z // 2
     few = part // n_zl
-    spread = jnp.swapaxes(layer.reshape(2, n_zl, few, count), 0, 1).reshape(n_z, few, count)
+    spread = pl.pallas_call(
+        layer_kernel,
+        out_shape=jax.ShapeDtypeStruct((n_z, few, count), f32),
+        in_specs=[VMEM],
+        out_specs=VMEM,
+        compiler_params=PARAMS,
+        name="layer",
+    )(parts)
     summed = jnp.sum(lax.all_to_all(spread, ("zl", "zh"), 0, 0, tiled=True), axis=0)
     my_dev = lax.axis_index(("zh", "x", "y"))
     first = my_dev * share + core * part + lax.axis_index("zl") * few

time: 178 us -> 178 us (level)
  no operation moved by 1% of the time
where the time goes in v6:
time: 178 us; the launch traced here: 177 us
  blocking collectives  114 us (64%)
  Pallas kernels  28.8 us (16%)
  starting transfers between devices  16.9 us (9%)
  waiting for transfers between devices  15.1 us (8%)
    all_to_all x1, blocking collectives, on_device(): slots = lax.all_to_all(packed, ('zl', 'zh'), 0, 0, tiled=True)  34.4 us
    all_to_all x1, blocking collectives, on_device(): lax.all_to_all(wide, ('x', 'y'), 0, 0, tiled=True)  25.2 us
    pallas_call x1, Pallas kernels, on_device(): pl.pallas_call(main_kernel, out_shape=(jax.ShapeDtypeStruct((rows_dev, co...  22 us
    all_to_all x1, blocking collectives, on_device(): parts = lax.all_to_all(pair, ('x', 'y'), 0, 0, tiled=True)  19.2 us
    all_to_all x1, blocking collectives, on_device(): got = lax.all_to_all(sent, ('core', 'x', 'y'), 0, 0, tiled=True)  17.6 us
    all_to_all x1, waiting for transfers between devices, on_device(): lax.all_to_all(spread, ('zl', 'zh'), 0, 0, tiled=True)  12.1 us
    all_to_all x1, blocking collectives, on_device(): line = lax.all_to_all(line, 'zl', 0, 0, tiled=True).reshape(part, count)  11.9 us
    all_to_all x1, starting transfers between devices, on_device(): lax.all_to_all(spread, ('zl', 'zh'), 0, 0, tiled=True)  7.9 us
  transfers between devices with their start and end apart: 3, of which 3 were waited for; matrix products, arithmetic and copies ran while one was open for 0% of the time, Pallas kernels for 1%

profile of v6, /device:TPU:1, one launch (start us, length us, event | category | flops | bytes accessed | tf_op | source)
XLA Modules:
  0.0 177.4 jit_solution(13685865500695870691)
XLA Ops:
  0.6 2.8 %pick.1 = f32[32,4,128]{2,1,0:T(4,128)} custom-call(s32[1]{0:T(128)} %bitcast.1.base_ref, s32[1]{0:T(128)} %bitcast.core_ref, s32[1,512]{1,0:T(1,128)} %bitcast.8, f32[256,1280]{1,0:T(8,128)} %emb_ref.3, f32[256,512]{1,0:T(8,128)} %fac_ref.3), custom_call_target="tpu_custom_call" | custom-call | tf_op jit(solution)/shard_map/pick/pallas_call | solution.py:322
  3.5 17.6 %all_to_all.30 = f32[32,4,128]{2,1,0:T(4,128)S(1)} all-to-all(f32[32,4,128]{2,1,0:T(4,128)} %pick.1), channel_id=1, replica_groups=mesh['zl'=8,'core'=2,'zh'=2,'x'=4,'y'=4] {'core','x','y'}, dimensions={0} | all-to-all | bytes 131072 | tf_op jit(solution)/shard_map/all_to_all | solution.py:336
  21.1 34.4 %all_to_all.31 = f32[16,48,128]{2,1,0:T(8,128)S(1)} all-to-all(f32[16,48,128]{2,1,0:T(8,128)S(1)} %broadcast_in_dim.9), channel_id=1, replica_groups=mesh['zl'=8,'core'=2,'zh'=2,'x'=4,'y'=4] {'zl','zh'}, dimensions={0} | all-to-all | bytes 786432 | tf_op jit(solution)/shard_map/all_to_all | solution.py:339
  55.5 0.9 select.1
  56.4 0.2 broadcast_in_dim.10
  56.7 0.0 copy-start
  56.7 0.0 copy-start.1
  56.7 25.2 %all_to_all.32 = f32[16,56,512]{2,1,0:T(8,128)S(1)} all-to-all(f32[16,56,512]{2,1,0:T(8,128)S(1)} %broadcast_in_dim.10), channel_id=1, replica_groups=mesh['zl'=8,'core'=2,'zh'=2,'x'=4,'y'=4] {'x','y'}, dimensions={0} | all-to-all | bytes 3670016 | tf_op jit(solution)/shard_map/all_to_all | solution.py:349
  81.9 6.7 %collective-permute-start = (f32[896,512]{1,0:T(8,128)S(1)}, f32[896,512]{1,0:T(8,128)S(1)}, u32[]{:S(2)}, u32[]{:S(2)}) collective-permute-start(f32[896,512]{1,0:T(8,128)S(1)} %bitcast.5), channel_id=1, source_target_pairs={{0,32},{32,0},{1,33},{33,1},{2,34},{34,2},{3,35},{35,3},{4,36},{36... | collective-permute-start | bytes 5505032 | tf_op jit(solution)/shard_map/ppermute | solution.py:350
  88.6 0.0 copy-done
  88.6 2.5 %first.1 = (f32[768,512]{1,0:T(8,128)S(1)}, f32[768,512]{1,0:T(8,128)S(1)}, f32[8,512]{1,0:T(8,128)S(1)}) custom-call(s32[1]{0:T(128)} %bitcast.core_ref, f32[256,1280]{1,0:T(8,128)S(1)} %copy-done, f32[256,512]{1,0:T(8,128)S(1)} %copy-done.1, f32[896,512]{1,0:T(8,128)S(1)} %bitcast.6), custom_call_target="tpu_custom_call" | custom-call | flops 2113929216 | bytes 1835008 | tf_op jit(solution)/shard_map/first/pallas_call | solution.py:355
  91.1 0.7 collective-permute-done.other_ref
  91.8 22.0 %main.1 = (f32[256,512]{1,0:T(8,128)}, f32[16,2,16,512]{3,2,1,0:T(8,128)S(1)}, f32[16,2,16,512]{3,2,1,0:T(8,128)S(1)}) custom-call(s32[1]{0:T(128)} %bitcast.core_ref, f32[256,1280]{1,0:T(8,128)S(1)} %copy-done, f32[256,512]{1,0:T(8,128)S(1)} %copy-done.1, f32[896,512]{1,0:T(8,128)S(1)} %collective-permute-done.other_ref, ...), custom_call_target="tpu_custom_call" | custom-call | tf_op jit(solution)/shard_map/main/pallas_call | solution.py:370
  113.8 2.3 %collective-permute-start.1 = (f32[16,2,16,512]{3,2,1,0:T(8,128)S(1)}, f32[16,2,16,512]{3,2,1,0:T(8,128)S(1)}, u32[]{:S(2)}, u32[]{:S(2)}) collective-permute-start(f32[16,2,16,512]{3,2,1,0:T(8,128)S(1)} %get-tuple-element.13), channel_id=1, source_target_pairs={{0,32},{32,0},{1,33},{33,1},{2,34},{34,2},{3,35},{35,3},{4,36},{36... | collective-permute-start | bytes 3145736 | tf_op jit(solution)/shard_map/ppermute | solution.py:387
  116.1 2.3 %collective-permute-done.1 = f32[16,2,16,512]{3,2,1,0:T(8,128)S(1)} collective-permute-done((f32[16,2,16,512]{3,2,1,0:T(8,128)S(1)}, f32[16,2,16,512]{3,2,1,0:T(8,128)S(1)}, u32[]{:S(2)}, u32[]{:S(2)}) %collective-permute-start.1) | collective-permute-done | bytes 1048608 | tf_op jit(solution)/shard_map/ppermute | solution.py:387
  118.3 0.2 add.55
  118.5 19.2 %all_to_all.33.parts_ref = f32[16,2,16,512]{3,2,1,0:T(8,128)S(1)} all-to-all(f32[16,2,16,512]{3,2,1,0:T(8,128)S(1)} %add.55), channel_id=1, replica_groups=mesh['zl'=8,'core'=2,'zh'=2,'x'=4,'y'=4] {'x','y'}, dimensions={0} | all-to-all | bytes 2097152 | tf_op jit(solution)/shard_map/all_to_all | solution.py:388
  137.8 0.7 layer.1
  138.5 7.9 %all-to-all-start.4 = ((f32[16,2,512]{2,1,0:T(2,128)}), f32[16,2,512]{2,1,0:T(2,128)S(1)}, u32[]{:S(2)}, u32[]{:S(2)}) async-start(f32[16,2,512]{2,1,0:T(2,128)} %layer.1), calls=%async_computation.4 | async-start | bytes 131072 | tf_op jit(solution)/shard_map/all_to_all | solution.py:399
  146.4 12.1 %all-to-all-done.4 = f32[16,2,512]{2,1,0:T(2,128)S(1)} async-done(((f32[16,2,512]{2,1,0:T(2,128)}), f32[16,2,512]{2,1,0:T(2,128)S(1)}, u32[]{:S(2)}, u32[]{:S(2)}) %all-to-all-start.4) | async-done | bytes 65568 | tf_op jit(solution)/shard_map/all_to_all | solution.py:399
  158.5 0.1 fusion
  158.6 11.9 %all_to_all.34 = f32[8,2,512]{2,1,0:T(2,128)S(1)} all-to-all(f32[8,2,512]{2,1,0:T(2,128)S(1)} %broadcast_in_dim.11), channel_id=1, replica_groups=mesh['zl'=8,'core'=2,'zh'=2,'x'=4,'y'=4] {'zl'}, dimensions={0} | all-to-all | bytes 65536 | tf_op jit(solution)/shard_map/all_to_all | solution.py:405
  170.5 6.3 %all_gather.3 = f32[32,512]{1,0:T(8,128)S(1)} all-gather(f32[16,512]{1,0:T(8,128)S(1)} %reshape.59), channel_id=1, replica_groups=mesh['zl'=8,'core'=2,'zh'=2,'x'=4,'y'=4] {'core'}, dimensions={0}, use_global_device_ids=true | all-gather | bytes 98304 | tf_op jit(solution)/shard_map/all_gather | solution.py:406
  176.8 0.6 copy.6
  (9 shorter events, 0.1 us)
Async XLA Ops:
  56.7 31.9 %copy-start = (f32[256,1280]{1,0:T(8,128)S(1)}, f32[256,1280]{1,0:T(8,128)}, u32[]{:S(2)}) copy-start(f32[256,1280]{1,0:T(8,128)} %emb_ref.3) | copy-start | bytes 3932164
  56.7 31.9 %copy-start.1 = (f32[256,512]{1,0:T(8,128)S(1)}, f32[256,512]{1,0:T(8,128)}, u32[]{:S(2)}) copy-start(f32[256,512]{1,0:T(8,128)} %fac_ref.3) | copy-start | bytes 1572868
  81.9 9.9 %collective-permute-start = (f32[896,512]{1,0:T(8,128)S(1)}, f32[896,512]{1,0:T(8,128)S(1)}, u32[]{:S(2)}, u32[]{:S(2)}) collective-permute-start(f32[896,512]{1,0:T(8,128)S(1)} %bitcast.5), channel_id=1, source_target_pairs={{0,32},{32,0},{1,33},{33,1},{2,34},{34,2},{3,35},{35,3},{4,36},{36... | collective-permute-start | bytes 5505032 | tf_op jit(solution)/shard_map/ppermute | solution.py:350
  113.8 4.6 %collective-permute-start.1 = (f32[16,2,16,512]{3,2,1,0:T(8,128)S(1)}, f32[16,2,16,512]{3,2,1,0:T(8,128)S(1)}, u32[]{:S(2)}, u32[]{:S(2)}) collective-permute-start(f32[16,2,16,512]{3,2,1,0:T(8,128)S(1)} %get-tuple-element.13), channel_id=1, source_target_pairs={{0,32},{32,0},{1,33},{33,1},{2,34},{34,2},{3,35},{35,3},{4,36},{36... | collective-permute-start | bytes 3145736 | tf_op jit(solution)/shard_map/ppermute | solution.py:387
  138.5 20.0 %all-to-all-start.4 = ((f32[16,2,512]{2,1,0:T(2,128)}), f32[16,2,512]{2,1,0:T(2,128)S(1)}, u32[]{:S(2)}, u32[]{:S(2)}) async-start(f32[16,2,512]{2,1,0:T(2,128)} %layer.1), calls=%async_computation.4 | async-start | bytes 131072 | tf_op jit(solution)/shard_map/all_to_all | solution.py:399
